TPU v7x, 32 devices: a whole 2x2x4 slice. The times are simulated.
32 devices in a mesh: fsdp: 4 (over x, core), ctx: 8 (over z, y).
Axes of the slice: x: 2, y: 2, z: 4, core: 2. Of those that a mesh axis runs over, the one named last changes fastest.
Arguments:
- tokens: bfloat16 [8192, 1024], P(('fsdp', 'ctx')), may hold values from -6 to 6
- segments: int32 [8192], P(('fsdp', 'ctx')), may hold values from 0 to 2047, as said below
- positions: int32 [8192], P(('fsdp', 'ctx')), may hold values from 0 to 4095, as said below
- cotangent: bfloat16 [8192, 1024], P(('fsdp', 'ctx')), may hold values from -12 to 12
- qkv_weight: bfloat16 [1024, 3072], P('fsdp'), may hold values from -0.1875 to 0.1875
- qkv_bias: bfloat16 [3072], P('fsdp'), may hold values from -1.75 to 1.75
- dense_weight: bfloat16 [1024, 1024], P('fsdp'), may hold values from -2 to 2
- dense_bias: bfloat16 [1024], P('fsdp'), may hold values from -1.75 to 1.75
- up_weight: bfloat16 [1024, 4096], P('fsdp'), may hold values from -0.1875 to 0.1875
- up_bias: bfloat16 [4096], P('fsdp'), may hold values from -1.75 to 1.75
- down_weight: bfloat16 [4096, 1024], P('fsdp'), may hold values from -0.09375 to 0.09375
- down_bias: bfloat16 [1024], P('fsdp'), may hold values from -1.75 to 1.75
- norm1_gain: bfloat16 [1024], P('fsdp'), may hold values from 0.25 to 1.75
- norm1_bias: bfloat16 [1024], P('fsdp'), may hold values from -1.75 to 1.75
- norm2_gain: bfloat16 [1024], P('fsdp'), may hold values from 0.25 to 1.75
- norm2_bias: bfloat16 [1024], P('fsdp'), may hold values from -1.75 to 1.75
Outputs:
- layer_out: bfloat16 [8192, 1024], P(('fsdp', 'ctx'))
- grad_tokens: bfloat16 [8192, 1024], P(('fsdp', 'ctx'))
- grad_qkv_weight: float32 [1024, 3072], P('fsdp')
- grad_qkv_bias: float32 [3072], P('fsdp')
- grad_dense_weight: float32 [1024, 1024], P('fsdp')
- grad_dense_bias: float32 [1024], P('fsdp')
- grad_up_weight: float32 [1024, 4096], P('fsdp')
- grad_up_bias: float32 [4096], P('fsdp')
- grad_down_weight: float32 [4096, 1024], P('fsdp')
- grad_down_bias: float32 [1024], P('fsdp')
- grad_norm1_gain: float32 [1024], P('fsdp')
- grad_norm1_bias: float32 [1024], P('fsdp')
- grad_norm2_gain: float32 [1024], P('fsdp')
- grad_norm2_bias: float32 [1024], P('fsdp')
Inputs may be any that keep to these rules, and one draw needn't show every extreme that they name: `segments`: within each sequence (the 2048 tokens of one index of fsdp) the numbers start at 0 and never fall; one document begins within its first 256 tokens and ends within its last 256. Within a document the positions rise by one from token to token.
All inputs are finite; a program needn't handle non-finite values.
Results may differ from a plain program's by a relative error of at most 0.024.
Values may be sent and summed in bfloat16 or wider, within the bound.
A program may use at most 192 MiB of HBM per device.

v0:
```python
import math

import jax
import jax.numpy as jnp
from jax import lax
from jax.sharding import PartitionSpec as P

HD = 64
ROT = 16


masked_fill = -1e30
norm_eps = 1e-05


def passed_along(block, axis, distance):
    devices = range(lax.axis_size(axis))
    route = [(i - distance, i) for i in devices if i - distance in devices]
    return lax.ppermute(block, axis, route)


def from_behind(value, axis, steps):
    count = lax.axis_size(axis)
    pairs = [(source, (source + steps) % count) for source in range(count)]
    return lax.ppermute(value, axis, pairs)


def layer_norm(inputs, gain_vec, shift_vec):
    center = inputs - jnp.mean(inputs, axis=-1, keepdims=True)
    spread = jnp.mean(center * center, axis=-1, keepdims=True)
    return center * lax.rsqrt(spread + norm_eps) * gain_vec + shift_vec


def rotary_tables(places):
    half_rot = ROT // 2
    inverse = 10000.0 ** (-2.0 * jnp.arange(half_rot, dtype=jnp.float32) / ROT)
    angles = places.astype(jnp.float32)[:, None] * inverse[None, :]
    angles = jnp.concatenate([angles, angles], axis=1)
    return (jnp.cos(angles), jnp.sin(angles))


def rotate(head_part, cosine_table, sine_table):
    half_rot = ROT // 2
    rotated_part = head_part[..., :ROT]
    turned = jnp.concatenate([-rotated_part[..., half_rot:], rotated_part[..., :half_rot]], axis=-1)
    rotated_part = rotated_part * cosine_table[:, None, :] + turned * sine_table[:, None, :]
    return jnp.concatenate([rotated_part, head_part[..., ROT:]], axis=-1)


def exact_gelu(values):
    return jax.nn.gelu(values, approximate=False)


def left_product(left_arg, right_arg):
    return lax.dot_general(
        left_arg, right_arg, (((0,), (0,)), ((), ())), preferred_element_type=jnp.float32
    )


def right_product(left_arg, right_arg):
    return lax.dot_general(
        left_arg, right_arg, (((1,), (1,)), ((), ())), preferred_element_type=jnp.float32
    )


def body(
    tokens,
    segments,
    positions,
    cotangent,
    qkv_weight,
    qkv_bias,
    dense_weight,
    dense_bias,
    up_weight,
    up_bias,
    down_weight,
    down_bias,
    norm1_gain,
    norm1_bias,
    norm2_gain,
    norm2_bias,
):
    gathered = (
        lax.all_gather(qkv_weight, "fsdp", axis=0, tiled=True),
        lax.all_gather(qkv_bias, "fsdp", axis=0, tiled=True),
        lax.all_gather(dense_weight, "fsdp", axis=0, tiled=True),
        lax.all_gather(dense_bias, "fsdp", axis=0, tiled=True),
        lax.all_gather(up_weight, "fsdp", axis=0, tiled=True),
        lax.all_gather(up_bias, "fsdp", axis=0, tiled=True),
        lax.all_gather(down_weight, "fsdp", axis=0, tiled=True),
        lax.all_gather(down_bias, "fsdp", axis=0, tiled=True),
        lax.all_gather(norm1_gain, "fsdp", axis=0, tiled=True),
        lax.all_gather(norm1_bias, "fsdp", axis=0, tiled=True),
        lax.all_gather(norm2_gain, "fsdp", axis=0, tiled=True),
        lax.all_gather(norm2_bias, "fsdp", axis=0, tiled=True),
    )
    (
        w_qkv,
        b_qkv,
        w_dense,
        b_dense,
        w_up,
        b_up,
        w_down,
        b_down,
        gain_one,
        bias_one,
        gain_two,
        bias_two,
    ) = gathered
    doc_all = lax.all_gather(segments, "ctx", axis=0, tiled=True)
    rows = tokens.shape[0]
    width = tokens.shape[1]
    heads = width // HD
    score_scale = 1.0 / math.sqrt(HD)
    ctx_count = lax.axis_size("ctx")
    my_index = lax.axis_index("ctx")
    query_place = my_index * rows + jnp.arange(rows, dtype=jnp.int32)
    inputs = tokens.astype(jnp.float32)
    normed_one, norm_one_pull = jax.vjp(
        layer_norm, inputs, gain_one.astype(jnp.float32), bias_one.astype(jnp.float32)
    )
    normed_one = normed_one.astype(jnp.bfloat16)
    mixed_proj = jnp.dot(normed_one, w_qkv, preferred_element_type=jnp.float32) + b_qkv.astype(
        jnp.float32
    )
    mixed_proj = mixed_proj.reshape(rows, heads, 3, HD)
    cosine_table, sine_table = rotary_tables(positions)

    def turn_heads(head_part):
        return rotate(head_part, cosine_table, sine_table)

    query_rot, rotary_pull = jax.vjp(turn_heads, mixed_proj[:, :, 0])
    key_rot = turn_heads(mixed_proj[:, :, 1])
    queries = query_rot.astype(jnp.bfloat16)
    keys_own = key_rot.astype(jnp.bfloat16).reshape(rows, width)
    values_own = mixed_proj[:, :, 2].astype(jnp.bfloat16).reshape(rows, width)

    def key_mask(q_place, q_doc, key_start, key_count):
        key_place = key_start + jnp.arange(key_count, dtype=jnp.int32)
        key_doc = lax.dynamic_slice_in_dim(doc_all, key_start, key_count, 0)
        return ((key_place[None, :] <= q_place[:, None]) & (key_doc[None, :] == q_doc[:, None]))[
            None
        ]

    def score_block(q_rows, q_place, q_doc, key_block, key_start, key_count):
        scores = (
            jnp.einsum("qhd,khd->hqk", q_rows, key_block, preferred_element_type=jnp.float32)
            * score_scale
        )
        return (scores, key_mask(q_place, q_doc, key_start, key_count))

    start_stats = (
        jnp.full((heads, rows), masked_fill, jnp.float32),
        jnp.zeros((heads, rows), jnp.float32),
    )

    def exp_block(scores, visible, q_max):
        return jnp.where(visible, jnp.exp(jnp.where(visible, scores - q_max[..., None], 0.0)), 0.0)

    zero_weighted = jnp.zeros((rows, heads, HD), jnp.float32)
    shard_piece = lax.all_gather(keys_own, "ctx", axis=0, tiled=True)
    key_count = shard_piece.shape[0]
    block_rows = math.gcd(key_count, 512)
    key_blocks = shard_piece.reshape(key_count // block_rows, block_rows, heads, HD)

    def stats_one_block(block_index, running):
        key_start = block_index * block_rows
        row_max, row_sum = running
        scores, visible = score_block(
            queries, query_place, segments, key_blocks[block_index], key_start, block_rows
        )
        new_max = jnp.maximum(row_max, jnp.max(jnp.where(visible, scores, masked_fill), axis=-1))
        exp_terms = jnp.where(
            visible, jnp.exp(jnp.where(visible, scores - new_max[..., None], 0.0)), 0.0
        )
        return (new_max, row_sum * jnp.exp(row_max - new_max) + jnp.sum(exp_terms, axis=-1))

    row_max, row_sum = lax.fori_loop(0, key_count // block_rows, stats_one_block, start_stats)
    q_max = row_max
    key_piece = lax.all_gather(keys_own, "ctx", axis=0, tiled=True)
    value_piece = lax.all_gather(values_own, "ctx", axis=0, tiled=True)
    key_count = key_piece.shape[0]
    make_block_rows = math.gcd(key_count, 512)
    make_key_blocks = key_piece.reshape(key_count // make_block_rows, make_block_rows, heads, HD)
    value_blocks = value_piece.reshape(key_count // make_block_rows, make_block_rows, heads, HD)

    def make_one_block(block_index, running):
        key_start = block_index * make_block_rows
        scores, visible = score_block(
            queries, query_place, segments, make_key_blocks[block_index], key_start, make_block_rows
        )
        exp_terms = exp_block(scores, visible, q_max).astype(jnp.bfloat16)
        return running + jnp.einsum(
            "hqk,khd->qhd", exp_terms, value_blocks[block_index], preferred_element_type=jnp.float32
        )

    weighted = lax.fori_loop(0, key_count // make_block_rows, make_one_block, zero_weighted)
    totals = jnp.transpose(row_sum)[:, :, None]
    context = weighted / totals
    context_low = context.astype(jnp.bfloat16).reshape(rows, width)
    attended = jnp.dot(context_low, w_dense, preferred_element_type=jnp.float32) + b_dense.astype(
        jnp.float32
    )
    normed_two, norm_two_pull = jax.vjp(
        layer_norm, inputs, gain_two.astype(jnp.float32), bias_two.astype(jnp.float32)
    )
    normed_two = normed_two.astype(jnp.bfloat16)
    up_proj = jnp.dot(normed_two, w_up, preferred_element_type=jnp.float32) + b_up.astype(
        jnp.float32
    )
    active, gelu_pull = jax.vjp(exact_gelu, up_proj)
    active = active.astype(jnp.bfloat16)
    mlp_out = jnp.dot(active, w_down, preferred_element_type=jnp.float32) + b_down.astype(
        jnp.float32
    )
    layer_out = (inputs + attended + mlp_out).astype(jnp.bfloat16)
    grad_out = cotangent.astype(jnp.float32)
    grad_down_w = left_product(active, cotangent)
    grad_down_b = jnp.sum(grad_out, axis=0)
    grad_dense_w = left_product(context_low, cotangent)
    grad_dense_b = jnp.sum(grad_out, axis=0)
    grad_active = right_product(cotangent, w_down)
    grad_up = gelu_pull(grad_active)[0].astype(jnp.bfloat16)
    grad_up_w = left_product(normed_two, grad_up)
    grad_up_b = jnp.sum(grad_up.astype(jnp.float32), axis=0)
    grad_normed_two = right_product(grad_up, w_up)
    grad_context = right_product(cotangent, w_dense).reshape(rows, heads, HD)
    grad_weighted = (grad_context / totals).astype(jnp.bfloat16)
    correction = jnp.transpose(jnp.sum(grad_context * context, axis=-1)) / row_sum

    def back_piece(carry_state, query_side, key_piece, value_piece, query_anchor, key_anchor):
        q_rows, q_grad_weighted, q_max, q_correction = query_side
        q_place = query_anchor * rows + jnp.arange(rows, dtype=jnp.int32)
        q_doc = lax.dynamic_slice_in_dim(doc_all, query_anchor * rows, rows, 0)
        block_rows = math.gcd(rows, 512)
        key_blocks = key_piece.reshape(rows // block_rows, block_rows, heads, HD)
        value_blocks = value_piece.reshape(rows // block_rows, block_rows, heads, HD)

        def back_one_block(block_index, running):
            key_start = key_anchor * rows + block_index * block_rows
            grad_query, grad_key, grad_value = running
            scores, visible = score_block(
                q_rows, q_place, q_doc, key_blocks[block_index], key_start, block_rows
            )
            exp_terms = exp_block(scores, visible, q_max)
            part_value = jnp.einsum(
                "hqk,qhd->khd",
                exp_terms.astype(jnp.bfloat16),
                q_grad_weighted,
                preferred_element_type=jnp.float32,
            )
            grad_terms = jnp.einsum(
                "qhd,khd->hqk",
                q_grad_weighted,
                value_blocks[block_index],
                preferred_element_type=jnp.float32,
            )
            grad_scores = (exp_terms * (grad_terms - q_correction[..., None])).astype(jnp.bfloat16)
            grad_query = (
                grad_query
                + jnp.einsum(
                    "hqk,khd->qhd",
                    grad_scores,
                    key_blocks[block_index],
                    preferred_element_type=jnp.float32,
                )
                * score_scale
            )
            part_key = (
                jnp.einsum("hqk,qhd->khd", grad_scores, q_rows, preferred_element_type=jnp.float32)
                * score_scale
            )
            grad_key = grad_key + part_key.reshape(block_rows, width)
            grad_value = grad_value + part_value.reshape(block_rows, width)
            return (grad_query, grad_key, grad_value)

        return lax.fori_loop(0, rows // block_rows, back_one_block, carry_state)

    own_query_side = (queries, grad_weighted, row_max, correction)
    zero_grads = jnp.zeros((rows, width), jnp.float32)
    first_state = back_piece(
        (jnp.zeros((rows, heads, HD), jnp.float32), zero_grads, zero_grads),
        own_query_side,
        keys_own,
        values_own,
        my_index,
        my_index,
    )

    def next_turn(turn_index, carry_state):
        grad_query, grad_key, grad_value, key_held, value_held = carry_state
        key_held, value_held = passed_along((key_held, value_held), "ctx", 1)
        grad_key, grad_value = (
            from_behind(grad_key.astype(jnp.bfloat16), "ctx", 1).astype(grad_key.dtype),
            from_behind(grad_value.astype(jnp.bfloat16), "ctx", 1).astype(grad_value.dtype),
        )
        anchor = (my_index - turn_index) % ctx_count
        grad_query, grad_key, grad_value = back_piece(
            (grad_query, grad_key, grad_value),
            own_query_side,
            key_held,
            value_held,
            my_index,
            anchor,
        )
        return (grad_query, grad_key, grad_value, key_held, value_held)

    cycle_state = lax.fori_loop(
        1,
        ctx_count,
        next_turn,
        (first_state[0], first_state[1], first_state[2], keys_own, values_own),
    )
    grad_query = cycle_state[0]
    grad_key, grad_value = (
        from_behind(cycle_state[1].astype(jnp.bfloat16), "ctx", 1).astype(jnp.float32),
        from_behind(cycle_state[2].astype(jnp.bfloat16), "ctx", 1).astype(jnp.float32),
    )
    grad_query_pre = rotary_pull(grad_query)[0]
    grad_key_pre = rotary_pull(grad_key.reshape(rows, heads, HD))[0]
    grad_mixed = jnp.stack(
        [grad_query_pre, grad_key_pre, grad_value.reshape(rows, heads, HD)], axis=2
    )
    grad_mixed = grad_mixed.reshape(rows, 3 * width).astype(jnp.bfloat16)
    grad_qkv_w = left_product(normed_one, grad_mixed)
    grad_qkv_b = jnp.sum(grad_mixed.astype(jnp.float32), axis=0)
    grad_normed_one = right_product(grad_mixed, w_qkv)
    input_one, grad_gain_one, grad_bias_one = norm_one_pull(grad_normed_one)
    input_two, grad_gain_two, grad_bias_two = norm_two_pull(grad_normed_two)
    grad_tokens = (grad_out + input_one + input_two).astype(jnp.bfloat16)
    (
        part_qkv_w,
        part_qkv_b,
        part_dense_w,
        part_dense_b,
        part_up_w,
        part_up_b,
        part_down_w,
        part_down_b,
        part_gain_one,
        part_bias_one,
        part_gain_two,
        part_bias_two,
    ) = (
        lax.psum_scatter(
            grad_qkv_w.astype(jnp.bfloat16), "fsdp", scatter_dimension=0, tiled=True
        ).astype(jnp.float32),
        lax.psum_scatter(
            grad_qkv_b.astype(jnp.bfloat16), "fsdp", scatter_dimension=0, tiled=True
        ).astype(jnp.float32),
        lax.psum_scatter(
            grad_dense_w.astype(jnp.bfloat16), "fsdp", scatter_dimension=0, tiled=True
        ).astype(jnp.float32),
        lax.psum_scatter(
            grad_dense_b.astype(jnp.bfloat16), "fsdp", scatter_dimension=0, tiled=True
        ).astype(jnp.float32),
        lax.psum_scatter(
            grad_up_w.astype(jnp.bfloat16), "fsdp", scatter_dimension=0, tiled=True
        ).astype(jnp.float32),
        lax.psum_scatter(
            grad_up_b.astype(jnp.bfloat16), "fsdp", scatter_dimension=0, tiled=True
        ).astype(jnp.float32),
        lax.psum_scatter(
            grad_down_w.astype(jnp.bfloat16), "fsdp", scatter_dimension=0, tiled=True
        ).astype(jnp.float32),
        lax.psum_scatter(
            grad_down_b.astype(jnp.bfloat16), "fsdp", scatter_dimension=0, tiled=True
        ).astype(jnp.float32),
        lax.psum_scatter(
            grad_gain_one.astype(jnp.bfloat16), "fsdp", scatter_dimension=0, tiled=True
        ).astype(jnp.float32),
        lax.psum_scatter(
            grad_bias_one.astype(jnp.bfloat16), "fsdp", scatter_dimension=0, tiled=True
        ).astype(jnp.float32),
        lax.psum_scatter(
            grad_gain_two.astype(jnp.bfloat16), "fsdp", scatter_dimension=0, tiled=True
        ).astype(jnp.float32),
        lax.psum_scatter(
            grad_bias_two.astype(jnp.bfloat16), "fsdp", scatter_dimension=0, tiled=True
        ).astype(jnp.float32),
    )
    reduced = (
        lax.psum(part_qkv_w.astype(jnp.bfloat16), "ctx").astype(jnp.float32),
        lax.psum(part_qkv_b.astype(jnp.bfloat16), "ctx").astype(jnp.float32),
        lax.psum(part_dense_w.astype(jnp.bfloat16), "ctx").astype(jnp.float32),
        lax.psum(part_dense_b.astype(jnp.bfloat16), "ctx").astype(jnp.float32),
        lax.psum(part_up_w.astype(jnp.bfloat16), "ctx").astype(jnp.float32),
        lax.psum(part_up_b.astype(jnp.bfloat16), "ctx").astype(jnp.float32),
        lax.psum(part_down_w.astype(jnp.bfloat16), "ctx").astype(jnp.float32),
        lax.psum(part_down_b.astype(jnp.bfloat16), "ctx").astype(jnp.float32),
        lax.psum(part_gain_one.astype(jnp.bfloat16), "ctx").astype(jnp.float32),
        lax.psum(part_bias_one.astype(jnp.bfloat16), "ctx").astype(jnp.float32),
        lax.psum(part_gain_two.astype(jnp.bfloat16), "ctx").astype(jnp.float32),
        lax.psum(part_bias_two.astype(jnp.bfloat16), "ctx").astype(jnp.float32),
    )
    return (
        layer_out,
        grad_tokens,
        reduced[0],
        reduced[1],
        reduced[2],
        reduced[3],
        reduced[4],
        reduced[5],
        reduced[6],
        reduced[7],
        reduced[8],
        reduced[9],
        reduced[10],
        reduced[11],
    )


def solution(mesh):
    return jax.shard_map(
        body,
        mesh=mesh,
        in_specs=(
            P(("fsdp", "ctx"), None),
            P(("fsdp", "ctx")),
            P(("fsdp", "ctx")),
            P(("fsdp", "ctx"), None),
            P("fsdp", None),
            P("fsdp"),
            P("fsdp", None),
            P("fsdp"),
            P("fsdp", None),
            P("fsdp"),
            P("fsdp", None),
            P("fsdp"),
            P("fsdp"),
            P("fsdp"),
            P("fsdp"),
            P("fsdp"),
        ),
        out_specs=(
            P(("fsdp", "ctx"), None),
            P(("fsdp", "ctx"), None),
            P("fsdp", None),
            P("fsdp"),
            P("fsdp", None),
            P("fsdp"),
            P("fsdp", None),
            P("fsdp"),
            P("fsdp", None),
            P("fsdp"),
            P("fsdp"),
            P("fsdp"),
            P("fsdp"),
            P("fsdp"),
        ),
        check_vma=False,
    )
```

profile of v0, /device:TPU:0, one launch (start us, length us, event | category | flops | bytes accessed | tf_op | source)
XLA Modules:
  0.0 1074.3 jit_solution(10513227632681522788)
XLA Ops:
  30.3 28.4 %all-gather.15.cloned.1.call-done = bf16[1024,3072]{1,0:T(8,128)(2,1)} async-done(((bf16[256,3072]{1,0:T(8,128)(2,1)}), bf16[1024,3072]{1,0:T(8,128)(2,1)}) %all-gather.15.cloned.1.call-update) | async-done | bytes 6291472 | tf_op jit(solution)/shard_map/all_gather | solution.py:85
  58.7 6.6 convolution_add_fusion.1
  88.3 20.7 %all-gather.3 = s32[8,1,256]{2,1,0:T(1,128)S(1)} all-gather(s32[1,1,256]{2,1,0:T(1,128)S(1)} %bitcast.225), channel_id=1, replica_groups=mesh['fsdp'=4,'ctx'=8] {'ctx'}, dimensions={0}, use_global_device_ids=true | all-gather | bytes 9216 | tf_op jit(solution)/shard_map/all_gather | solution.py:112
  112.6 48.1 %all-gather.17.cloned.1.call-done = bf16[2048,1024]{0,1:T(8,128)(2,1)} async-done(((bf16[256,1024]{0,1:T(8,128)(2,1)}), bf16[2048,1024]{0,1:T(8,128)(2,1)}) %all-gather.17.cloned.1.call-update) | async-done | bytes 4194320 | tf_op jit(solution)/shard_map/all_gather | solution.py:183
  160.7 7.8 reshape.472
  173.9 62.5 %all-gather.19.cloned.1.call-done = bf16[2048,1024]{0,1:T(8,128)(2,1)} async-done(((bf16[256,1024]{0,1:T(8,128)(2,1)}), bf16[2048,1024]{0,1:T(8,128)(2,1)}) %all-gather.19.cloned.1.call-update) | async-done | bytes 4194320 | tf_op jit(solution)/shard_map/all_gather | solution.py:182
  236.4 7.9 reshape.473
  250.1 43.3 %while.76 = (s32[]{:T(128)}, f32[16,256]{1,0:T(8,128)S(1)}, f32[16,256]{1,0:T(8,128)S(1)}, s32[2048]{0:T(1024)S(1)}, s32[256]{0:T(256)S(1)}, /*index=5*/bf16[4,5...) while((s32[]{:T(128)}, f32[16,256]{1,0:T(8,128)S(1)}, ...), condition=%wide.region_5.6_spmd.clone, body=%wide.region_2.5_spmd.clone.sunk | while | flops 285627136 | bytes 18969796 | solution.py:180
  293.3 24.0 %while.77 = (s32[]{:T(128)}, f32[256,16,64]{0,2,1:T(8,128)}, bf16[4,512,16,64]{1,3,2,0:T(8,128)(2,1)}, s32[2048]{0:T(1024)S(1)}, s32[256]{0:T(256)S(1)}, /*index...) while((s32[]{:T(128)}, f32[256,16,64]{0,2,1:T(8,128)}, ...), condition=%wide.region_7.8_spmd.clone, body=%wide.region_6.7_spmd.clone.sunk | while | flops 548274944 | bytes 5012168 | solution.py:199
  322.5 7.9 convolution_add_fusion
  330.4 23.6 %all-gather.25.cloned.1.call-done = bf16[4096,1024]{1,0:T(8,128)(2,1)} async-done(((bf16[1024,1024]{1,0:T(8,128)(2,1)}), bf16[4096,1024]{1,0:T(8,128)(2,1)}) %all-gather.25.cloned.1.call-update) | async-done | bytes 8388624 | tf_op jit(solution)/shard_map/all_gather | solution.py:91
  354.0 16.4 %fusion.98 = (bf16[4096]{0:T(1024)(128)(2,1)}, bf16[256,4096]{1,0:T(8,128)(2,1)S(1)}, f32[256,4096]{1,0:T(8,128)}) fusion(f32[256,4096]{1,0:T(8,128)} %convolution_add_fusion, bf16[256,1024]{1,0:T(8,128)(2,1)S(1)} %copy-done.1, bf16[4096,1024]{1,0:T(8,128)(2,1)} %all-gather.25.cloned.1.call-done), kind=kOutput, calls=%fused_computation.167 | convolution fusion | flops 2224025600 | bytes 19406848 | tf_op jit(solution)/shard_map/dot_general | solution.py:61
  400.9 348.3 %while.75 = (s32[]{:T(128)}, f32[256,16,64]{0,2,1:T(8,128)S(1)}, bf16[256,1024]{0,1:T(8,128)(2,1)}, bf16[256,1024]{0,1:T(8,128)(2,1)}, bf16[256,1024]{0,1:T(8,12...) while((s32[]{:T(128)}, f32[256,16,64]{0,2,1:T(8,128)S(1)}, ...), condition=%wide.region_10.11_spmd, body=%wide.region_9.10_spmd.sunk | while | flops 686227968 | bytes 43770404 | solution.py:310
  417.9 10.5 collective-permute-done.1
  432.6 6.9 collective-permute-done.2
  469.9 10.5 collective-permute-done.1
  484.7 6.9 collective-permute-done.2
  521.1 10.5 collective-permute-done.1
  535.9 7.0 collective-permute-done.2
  572.1 10.5 collective-permute-done.1
  586.9 7.0 collective-permute-done.2
  622.4 10.5 collective-permute-done.1
  637.2 7.0 collective-permute-done.2
  671.7 10.5 collective-permute-done.1
  686.5 7.0 collective-permute-done.2
  720.1 10.5 collective-permute-done.1
  756.2 10.8 %collective-permute-done.4 = bf16[256,1024]{0,1:T(8,128)(2,1)S(1)} collective-permute-done((bf16[256,1024]{0,1:T(8,128)(2,1)}, bf16[256,1024]{0,1:T(8,128)(2,1)S(1)}, u32[]{:S(2)}, u32[]{:S(2)}) %collective-permute-start.4) | collective-permute-done | bytes 524320 | tf_op jit(solution)/shard_map/ppermute | solution.py:25
  779.3 58.5 %reduce-scatter.5.cloned.1.call-done = bf16[256,3072]{1,0:T(8,128)(2,1)} async-done(((bf16[1024,3072]{1,0:T(8,128)(2,1)}), bf16[256,3072]{1,0:T(8,128)(2,1)}) %reduce-scatter.5.cloned.1.call-update) | async-done | bytes 1572880 | tf_op jit(solution)/shard_map/reduce_scatter | solution.py:347
  850.7 7.5 fusion.106
  872.1 11.2 %all-reduce.17 = (bf16[3072]{0:T(1024)(128)(2,1)S(1)}, bf16[1024]{0:T(1024)(128)(2,1)S(1)}, bf16[4096]{0:T(1024)(128)(2,1)S(1)}, bf16[1024]{0:T(1024)(128)(2,1)S...) all-reduce(bf16[3072]{0:T(1024)(128)(2,1)S(1)} %reduce_sum.171, ...), channel_id=3, replica_groups=mesh['fsdp'=4,'ctx'=8] {'fsdp'}, use_global_device_ids=true, to_apply=%region_18.19.clone | all-reduce | flops 12288 | bytes 49152
  883.8 23.1 %all-reduce.15 = (bf16[768]{0:T(1024)(128)(2,1)S(1)}, bf16[256]{0:T(256)(128)(2,1)S(1)}, bf16[1024]{0:T(1024)(128)(2,1)S(1)}, bf16[256]{0:T(256)(128)(2,1)S(1)},...) all-reduce(bf16[768]{0:T(1024)(128)(2,1)S(1)} %dynamic-slice.3, ...), channel_id=1, replica_groups=mesh['fsdp'=4,'ctx'=8] {'ctx'}, use_global_device_ids=true, to_apply=%region_19.20 | all-reduce | flops 3072 | bytes 12288 | tf_op jit(solution)/shard_map/psum | solution.py:386
  913.4 144.0 %all-reduce.20.cloned.1.call-done = (bf16[256,3072]{1,0:T(8,128)(2,1)}, bf16[256,1024]{1,0:T(8,128)(2,1)}, bf16[256,4096]{1,0:T(8,128)(2,1)}, bf16[1024,1024]{1,0:T(8,128)(2,1)}) async-done(((bf16[256,3072]{1,0:T(8,128)(2,1)}, bf16[256,1024]{1,0:T(8,128)(2,1)}, bf16[256,4096]{1,0:T(8,128)(2,1)}, bf16[1024,1024]{1,0:T(8,128)(2,1)}), (bf16[256,3072]{1,0:T(8,128)(2,1)}, bf16[256,1024]{1,0:T(8,128)(2,1)}, ...) | async-done | bytes 6291472 | tf_op jit(solution)/shard_map/psum | solution.py:385
  (467 shorter events, 456.7 us)
Async XLA Ops:
  7.2 51.5 %all-gather.15.cloned.1.call-start = ((), (), s32[]{:S(2)}) async-start(), calls=%async_computation.4 | async-start | bytes 7864320 | tf_op jit(solution)/shard_map/all_gather | solution.py:85
  7.9 101.1 %all-gather.21.cloned.1.call-start = ((), (), s32[]{:S(2)}) async-start(), calls=%async_computation.7 | async-start | bytes 2621440 | tf_op jit(solution)/shard_map/all_gather | solution.py:87
  8.7 152.0 %all-gather.17.cloned.1.call-start = ((), (), s32[]{:S(2)}) async-start(), calls=%async_computation.5 | async-start | bytes 4718592 | tf_op jit(solution)/shard_map/all_gather | solution.py:183
  68.9 167.5 %all-gather.19.cloned.1.call-start = ((), (), s32[]{:S(2)}) async-start(), calls=%async_computation.6 | async-start | bytes 4718592 | tf_op jit(solution)/shard_map/all_gather | solution.py:182
  71.7 250.8 %all-gather.23.cloned.1.call-start = ((), (), s32[]{:S(2)}) async-start(), calls=%async_computation.8 | async-start | bytes 10485760 | tf_op jit(solution)/shard_map/all_gather | solution.py:89
  72.3 281.8 %all-gather.25.cloned.1.call-start = ((), (), s32[]{:S(2)}) async-start(), calls=%async_computation.9 | async-start | bytes 10485760 | tf_op jit(solution)/shard_map/all_gather | solution.py:91
  72.8 706.4 %reduce-scatter.7.cloned.1.call-start = ((), (), s32[]{:S(2)}) async-start(), calls=%async_computation.11 | async-start | bytes 2621440 | tf_op jit(solution)/shard_map/reduce_scatter | solution.py:353
  322.1 457.1 %reduce-scatter.9.cloned.1.call-start = ((), (), s32[]{:S(2)}) async-start(), calls=%async_computation.12 | async-start | bytes 10485760 | tf_op jit(solution)/shard_map/reduce_scatter | solution.py:359
  377.6 401.6 %reduce-scatter.11.cloned.1.call-start = ((), (), s32[]{:S(2)}) async-start(), calls=%async_computation.13 | async-start | bytes 10485760 | tf_op jit(solution)/shard_map/reduce_scatter | solution.py:365
  391.2 446.5 %reduce-scatter.5.cloned.1.call-start = ((), (), s32[]{:S(2)}) async-start(), calls=%async_computation.10 | async-start | bytes 7864320 | tf_op jit(solution)/shard_map/reduce_scatter | solution.py:347
  404.6 23.8 %collective-permute-start.1 = (bf16[256,1024]{0,1:T(8,128)(2,1)}, bf16[256,1024]{0,1:T(8,128)(2,1)}, u32[]{:S(2)}, u32[]{:S(2)}) collective-permute-start(bf16[256,1024]{0,1:T(8,128)(2,1)} %get-tuple-element.1268), channel_id=1, source_target_pairs={{0,1},{1,2},{2,3},{3,4},{4,5},{5,6},{6,7},{8,9},{9,10},{10,11},{11... | collective-permute-start | bytes 1572872 | tf_op jit(solution)/shard_map/while/body/eval_jaxpr/ppermute | solution.py:19
  408.7 30.8 %collective-permute-start.2 = (bf16[256,1024]{0,1:T(8,128)(2,1)}, bf16[256,1024]{0,1:T(8,128)(2,1)}, u32[]{:S(2)}, u32[]{:S(2)}) collective-permute-start(bf16[256,1024]{0,1:T(8,128)(2,1)} %get-tuple-element.1265), channel_id=1, source_target_pairs={{0,1},{1,2},{2,3},{3,4},{4,5},{5,6},{6,7},{7,0},{8,9},{9,10},{10,1... | collective-permute-start | bytes 1572872 | tf_op jit(solution)/shard_map/while/body/eval_jaxpr/ppermute | solution.py:25
  409.4 40.6 %collective-permute-start.3 = (bf16[256,1024]{0,1:T(8,128)(2,1)}, bf16[256,1024]{0,1:T(8,128)(2,1)}, u32[]{:S(2)}, u32[]{:S(2)}) collective-permute-start(bf16[256,1024]{0,1:T(8,128)(2,1)} %get-tuple-element.1266), channel_id=1, source_target_pairs={{0,1},{1,2},{2,3},{3,4},{4,5},{5,6},{6,7},{7,0},{8,9},{9,10},{10,1... | collective-permute-start | bytes 1572872 | tf_op jit(solution)/shard_map/while/body/eval_jaxpr/ppermute | solution.py:25
  456.5 23.9 %collective-permute-start.1 = (bf16[256,1024]{0,1:T(8,128)(2,1)}, bf16[256,1024]{0,1:T(8,128)(2,1)}, u32[]{:S(2)}, u32[]{:S(2)}) collective-permute-start(bf16[256,1024]{0,1:T(8,128)(2,1)} %get-tuple-element.1268), channel_id=1, source_target_pairs={{0,1},{1,2},{2,3},{3,4},{4,5},{5,6},{6,7},{8,9},{9,10},{10,11},{11... | collective-permute-start | bytes 1572872 | tf_op jit(solution)/shard_map/while/body/eval_jaxpr/ppermute | solution.py:19
  461.6 30.1 %collective-permute-start.2 = (bf16[256,1024]{0,1:T(8,128)(2,1)}, bf16[256,1024]{0,1:T(8,128)(2,1)}, u32[]{:S(2)}, u32[]{:S(2)}) collective-permute-start(bf16[256,1024]{0,1:T(8,128)(2,1)} %get-tuple-element.1265), channel_id=1, source_target_pairs={{0,1},{1,2},{2,3},{3,4},{4,5},{5,6},{6,7},{7,0},{8,9},{9,10},{10,1... | collective-permute-start | bytes 1572872 | tf_op jit(solution)/shard_map/while/body/eval_jaxpr/ppermute | solution.py:25
  461.6 39.6 %collective-permute-start.3 = (bf16[256,1024]{0,1:T(8,128)(2,1)}, bf16[256,1024]{0,1:T(8,128)(2,1)}, u32[]{:S(2)}, u32[]{:S(2)}) collective-permute-start(bf16[256,1024]{0,1:T(8,128)(2,1)} %get-tuple-element.1266), channel_id=1, source_target_pairs={{0,1},{1,2},{2,3},{3,4},{4,5},{5,6},{6,7},{7,0},{8,9},{9,10},{10,1... | collective-permute-start | bytes 1572872 | tf_op jit(solution)/shard_map/while/body/eval_jaxpr/ppermute | solution.py:25
  507.7 23.9 %collective-permute-start.1 = (bf16[256,1024]{0,1:T(8,128)(2,1)}, bf16[256,1024]{0,1:T(8,128)(2,1)}, u32[]{:S(2)}, u32[]{:S(2)}) collective-permute-start(bf16[256,1024]{0,1:T(8,128)(2,1)} %get-tuple-element.1268), channel_id=1, source_target_pairs={{0,1},{1,2},{2,3},{3,4},{4,5},{5,6},{6,7},{8,9},{9,10},{10,11},{11... | collective-permute-start | bytes 1572872 | tf_op jit(solution)/shard_map/while/body/eval_jaxpr/ppermute | solution.py:19
  513.6 29.2 %collective-permute-start.2 = (bf16[256,1024]{0,1:T(8,128)(2,1)}, bf16[256,1024]{0,1:T(8,128)(2,1)}, u32[]{:S(2)}, u32[]{:S(2)}) collective-permute-start(bf16[256,1024]{0,1:T(8,128)(2,1)} %get-tuple-element.1265), channel_id=1, source_target_pairs={{0,1},{1,2},{2,3},{3,4},{4,5},{5,6},{6,7},{7,0},{8,9},{9,10},{10,1... | collective-permute-start | bytes 1572872 | tf_op jit(solution)/shard_map/while/body/eval_jaxpr/ppermute | solution.py:25
  513.6 37.8 %collective-permute-start.3 = (bf16[256,1024]{0,1:T(8,128)(2,1)}, bf16[256,1024]{0,1:T(8,128)(2,1)}, u32[]{:S(2)}, u32[]{:S(2)}) collective-permute-start(bf16[256,1024]{0,1:T(8,128)(2,1)} %get-tuple-element.1266), channel_id=1, source_target_pairs={{0,1},{1,2},{2,3},{3,4},{4,5},{5,6},{6,7},{7,0},{8,9},{9,10},{10,1... | collective-permute-start | bytes 1572872 | tf_op jit(solution)/shard_map/while/body/eval_jaxpr/ppermute | solution.py:25
  558.7 23.9 %collective-permute-start.1 = (bf16[256,1024]{0,1:T(8,128)(2,1)}, bf16[256,1024]{0,1:T(8,128)(2,1)}, u32[]{:S(2)}, u32[]{:S(2)}) collective-permute-start(bf16[256,1024]{0,1:T(8,128)(2,1)} %get-tuple-element.1268), channel_id=1, source_target_pairs={{0,1},{1,2},{2,3},{3,4},{4,5},{5,6},{6,7},{8,9},{9,10},{10,11},{11... | collective-permute-start | bytes 1572872 | tf_op jit(solution)/shard_map/while/body/eval_jaxpr/ppermute | solution.py:19
  564.8 29.0 %collective-permute-start.2 = (bf16[256,1024]{0,1:T(8,128)(2,1)}, bf16[256,1024]{0,1:T(8,128)(2,1)}, u32[]{:S(2)}, u32[]{:S(2)}) collective-permute-start(bf16[256,1024]{0,1:T(8,128)(2,1)} %get-tuple-element.1265), channel_id=1, source_target_pairs={{0,1},{1,2},{2,3},{3,4},{4,5},{5,6},{6,7},{7,0},{8,9},{9,10},{10,1... | collective-permute-start | bytes 1572872 | tf_op jit(solution)/shard_map/while/body/eval_jaxpr/ppermute | solution.py:25
  564.8 36.8 %collective-permute-start.3 = (bf16[256,1024]{0,1:T(8,128)(2,1)}, bf16[256,1024]{0,1:T(8,128)(2,1)}, u32[]{:S(2)}, u32[]{:S(2)}) collective-permute-start(bf16[256,1024]{0,1:T(8,128)(2,1)} %get-tuple-element.1266), channel_id=1, source_target_pairs={{0,1},{1,2},{2,3},{3,4},{4,5},{5,6},{6,7},{7,0},{8,9},{9,10},{10,1... | collective-permute-start | bytes 1572872 | tf_op jit(solution)/shard_map/while/body/eval_jaxpr/ppermute | solution.py:25
  609.0 23.9 %collective-permute-start.1 = (bf16[256,1024]{0,1:T(8,128)(2,1)}, bf16[256,1024]{0,1:T(8,128)(2,1)}, u32[]{:S(2)}, u32[]{:S(2)}) collective-permute-start(bf16[256,1024]{0,1:T(8,128)(2,1)} %get-tuple-element.1268), channel_id=1, source_target_pairs={{0,1},{1,2},{2,3},{3,4},{4,5},{5,6},{6,7},{8,9},{9,10},{10,11},{11... | collective-permute-start | bytes 1572872 | tf_op jit(solution)/shard_map/while/body/eval_jaxpr/ppermute | solution.py:19
  615.1 29.0 %collective-permute-start.2 = (bf16[256,1024]{0,1:T(8,128)(2,1)}, bf16[256,1024]{0,1:T(8,128)(2,1)}, u32[]{:S(2)}, u32[]{:S(2)}) collective-permute-start(bf16[256,1024]{0,1:T(8,128)(2,1)} %get-tuple-element.1265), channel_id=1, source_target_pairs={{0,1},{1,2},{2,3},{3,4},{4,5},{5,6},{6,7},{7,0},{8,9},{9,10},{10,1... | collective-permute-start | bytes 1572872 | tf_op jit(solution)/shard_map/while/body/eval_jaxpr/ppermute | solution.py:25
  615.1 35.9 %collective-permute-start.3 = (bf16[256,1024]{0,1:T(8,128)(2,1)}, bf16[256,1024]{0,1:T(8,128)(2,1)}, u32[]{:S(2)}, u32[]{:S(2)}) collective-permute-start(bf16[256,1024]{0,1:T(8,128)(2,1)} %get-tuple-element.1266), channel_id=1, source_target_pairs={{0,1},{1,2},{2,3},{3,4},{4,5},{5,6},{6,7},{7,0},{8,9},{9,10},{10,1... | collective-permute-start | bytes 1572872 | tf_op jit(solution)/shard_map/while/body/eval_jaxpr/ppermute | solution.py:25
  658.3 23.9 %collective-permute-start.1 = (bf16[256,1024]{0,1:T(8,128)(2,1)}, bf16[256,1024]{0,1:T(8,128)(2,1)}, u32[]{:S(2)}, u32[]{:S(2)}) collective-permute-start(bf16[256,1024]{0,1:T(8,128)(2,1)} %get-tuple-element.1268), channel_id=1, source_target_pairs={{0,1},{1,2},{2,3},{3,4},{4,5},{5,6},{6,7},{8,9},{9,10},{10,11},{11... | collective-permute-start | bytes 1572872 | tf_op jit(solution)/shard_map/while/body/eval_jaxpr/ppermute | solution.py:19
  664.4 29.0 %collective-permute-start.2 = (bf16[256,1024]{0,1:T(8,128)(2,1)}, bf16[256,1024]{0,1:T(8,128)(2,1)}, u32[]{:S(2)}, u32[]{:S(2)}) collective-permute-start(bf16[256,1024]{0,1:T(8,128)(2,1)} %get-tuple-element.1265), channel_id=1, source_target_pairs={{0,1},{1,2},{2,3},{3,4},{4,5},{5,6},{6,7},{7,0},{8,9},{9,10},{10,1... | collective-permute-start | bytes 1572872 | tf_op jit(solution)/shard_map/while/body/eval_jaxpr/ppermute | solution.py:25
  664.4 35.0 %collective-permute-start.3 = (bf16[256,1024]{0,1:T(8,128)(2,1)}, bf16[256,1024]{0,1:T(8,128)(2,1)}, u32[]{:S(2)}, u32[]{:S(2)}) collective-permute-start(bf16[256,1024]{0,1:T(8,128)(2,1)} %get-tuple-element.1266), channel_id=1, source_target_pairs={{0,1},{1,2},{2,3},{3,4},{4,5},{5,6},{6,7},{7,0},{8,9},{9,10},{10,1... | collective-permute-start | bytes 1572872 | tf_op jit(solution)/shard_map/while/body/eval_jaxpr/ppermute | solution.py:25
  706.7 23.9 %collective-permute-start.1 = (bf16[256,1024]{0,1:T(8,128)(2,1)}, bf16[256,1024]{0,1:T(8,128)(2,1)}, u32[]{:S(2)}, u32[]{:S(2)}) collective-permute-start(bf16[256,1024]{0,1:T(8,128)(2,1)} %get-tuple-element.1268), channel_id=1, source_target_pairs={{0,1},{1,2},{2,3},{3,4},{4,5},{5,6},{6,7},{8,9},{9,10},{10,11},{11... | collective-permute-start | bytes 1572872 | tf_op jit(solution)/shard_map/while/body/eval_jaxpr/ppermute | solution.py:19
  712.8 28.4 %collective-permute-start.2 = (bf16[256,1024]{0,1:T(8,128)(2,1)}, bf16[256,1024]{0,1:T(8,128)(2,1)}, u32[]{:S(2)}, u32[]{:S(2)}) collective-permute-start(bf16[256,1024]{0,1:T(8,128)(2,1)} %get-tuple-element.1265), channel_id=1, source_target_pairs={{0,1},{1,2},{2,3},{3,4},{4,5},{5,6},{6,7},{7,0},{8,9},{9,10},{10,1... | collective-permute-start | bytes 1572872 | tf_op jit(solution)/shard_map/while/body/eval_jaxpr/ppermute | solution.py:25
  712.8 34.3 %collective-permute-start.3 = (bf16[256,1024]{0,1:T(8,128)(2,1)}, bf16[256,1024]{0,1:T(8,128)(2,1)}, u32[]{:S(2)}, u32[]{:S(2)}) collective-permute-start(bf16[256,1024]{0,1:T(8,128)(2,1)} %get-tuple-element.1266), channel_id=1, source_target_pairs={{0,1},{1,2},{2,3},{3,4},{4,5},{5,6},{6,7},{7,0},{8,9},{9,10},{10,1... | collective-permute-start | bytes 1572872 | tf_op jit(solution)/shard_map/while/body/eval_jaxpr/ppermute | solution.py:25
  779.1 278.2 %all-reduce.20.cloned.1.call-start = ((), (), s32[]{:S(2)}) async-start(), calls=%async_computation.14 | async-start | bytes 12582912 | tf_op jit(solution)/shard_map/psum | solution.py:385
  (80 other events, 2427.3 us)
Sparse Core Ops, SparseCore 0:
  9.6 49.0 all-gather.14
  60.3 22.6 all-gather.20
  85.6 75.0 all-gather.16
  163.1 73.1 all-gather.18
  237.8 56.4 all-gather.22
  295.7 58.2 all-gather.24
  356.5 31.4 reduce-scatter.6
  390.8 71.6 reduce-scatter.8
  465.1 71.7 reduce-scatter.10
  779.2 58.5 reduce-scatter.4
  842.2 215.0 all-reduce.19
where the time goes:
time: 1080 us; the launch traced here: 1070 us
  waiting for transfers between devices  545 us (50%)
  matrix products  174 us (16%)
  blocking collectives  97 us (9%)
  starting transfers between devices  96.6 us (9%)
  other arithmetic  77 us (7%)
  local copies, waits for them, and re-layouts  67.2 us (6%)
  between operations  16.9 us (2%)
    psum x1, waiting for transfers between devices, body(): lax.psum(part_qkv_w.astype(jnp.bfloat16), 'ctx').astype(jnp.float32)  144 us
    ppermute x14, waiting for transfers between devices, passed_along(): return lax.ppermute(block, axis, route)  100 us
    ppermute x16, waiting for transfers between devices, from_behind(): return lax.ppermute(value, axis, pairs)  77.6 us
    ppermute x14, starting transfers between devices, passed_along(): return lax.ppermute(block, axis, route)  73.1 us
    all_gather x1, waiting for transfers between devices, body(): key_piece = lax.all_gather(keys_own, 'ctx', axis=0, tiled=True)  62.5 us
    reduce_scatter x1, waiting for transfers between devices, body(): lax.psum_scatter(grad_qkv_w.astype(jnp.bfloat16), 'fsdp', scatter_dimensi...  58.5 us
    all_gather x1, waiting for transfers between devices, body(): value_piece = lax.all_gather(values_own, 'ctx', axis=0, tiled=True)  48.1 us
    dot_general x4, matrix products, right_product(): lax.dot_general(left_arg, right_arg, (((1,), (1,)), ((), ())), preferred_...  32.5 us
  transfers between devices with their start and end apart: 41, of which 34 were waited for; matrix products, arithmetic and copies ran while one was open for 28% of the time, Pallas kernels for 0%

commit v1 on v0

v1 whole, which is shorter than its diff:
```python
import functools
import math

import numpy as np
import jax, jax.numpy as jnp
from jax import lax
from jax.experimental import pallas as pl
from jax.experimental.pallas import tpu as pltpu
from jax.sharding import PartitionSpec as P

HD, ROT = 64, 16
f32, bf16 = jnp.float32, jnp.bfloat16
MESH = pl.DeviceIdType.MESH
vmem = pl.BlockSpec(memory_space=pltpu.VMEM)
hbm = pl.BlockSpec(memory_space=pl.ANY)
norm_eps = 1e-5
masked_fill = -1e30


def nn(a, b):
    return jnp.dot(a, b, preferred_element_type=f32)


def nt(a, b):
    return lax.dot_general(a, b, (((1,), (1,)), ((), ())), preferred_element_type=f32)


def tn(a, b):
    return lax.dot_general(a, b, (((0,), (0,)), ((), ())), preferred_element_type=f32)


def flipped(a, d, n):
    out, bit = 0, 1
    while bit < n:
        out = out + bit * ((a // bit + d // bit) % 2)
        bit *= 2
    return out


def kernel_p(pos, seg, g1, b1, g2, b2, dense, down, qkv, up, pk, vec):
    half, rows = ROT // 2, pos.shape[0]
    row = lax.broadcasted_iota(jnp.int32, (ROT, rows), 0)
    rate = jnp.zeros((ROT, rows), f32)
    for j in range(half):
        rate = jnp.where(row % half == j, float(np.float32(10000.0) ** np.float32(-2.0 * j / ROT)), rate)
    angle = rate * jnp.broadcast_to(pos[...].astype(f32).reshape(1, rows), (ROT, rows))
    pk[0:ROT, :] = jnp.where(row < half, jnp.cos(angle), jnp.sin(angle))
    pk[ROT:, :] = jnp.zeros((8, rows), f32)
    vec[...] = jnp.zeros_like(vec)

    def line(ref):
        return ref[...].astype(f32).reshape(1, ref.shape[0])

    for i, ref in enumerate((g1, b1, g2, b2, seg)):
        pk[ROT + i : ROT + i + 1, :] = line(ref)
    pk[ROT + 5 : ROT + 6, :] = line(dense) + line(down)
    vec[0:1, 0 : qkv.shape[0]] = line(qkv)
    vec[1:2, 0 : up.shape[0]] = line(up)


def call_p(pos, seg, g1, b1, g2, b2, dense, down, qkv, up):
    n = max(qkv.shape[0], up.shape[0])
    return pl.pallas_call(
        kernel_p,
        out_shape=(jax.ShapeDtypeStruct((24, pos.shape[0]), f32), jax.ShapeDtypeStruct((8, n), f32)),
        name="pack",
    )(pos, seg, g1, b1, g2, b2, dense, down, qkv, up)


def rotary_terms(pk):
    rest = pk[0:ROT, :]
    terms = []
    for _ in range(3):
        part = rest.astype(bf16)
        terms.append(part)
        rest = rest - part.astype(f32)
    return jnp.concatenate(terms + [jnp.ones_like(terms[0])], axis=0)


def rotary_pattern():
    e = np.zeros((64, 9 * 128), np.float32)
    for tile in range(3):
        for lane in range(128):
            col = tile * 128 + lane
            part, d = (col % 192) // HD, col % HD
            base = tile * 384 + lane
            if part == 2 or d >= ROT:
                e[48, base] = 1.0
                continue
            for term in range(3):
                e[term * 16 + d % 8, base] = 1.0
                if d < 8:
                    e[term * 16 + 8 + d, base + 128] = -1.0
                else:
                    e[term * 16 + d, base + 256] = 1.0
    return e


def turn(tile, table, t, sign):
    c = table[:, t * 384 : t * 384 + 128]
    up = table[:, t * 384 + 128 : t * 384 + 256]
    dn = table[:, t * 384 + 256 : t * 384 + 384]
    return tile * c + sign * (pltpu.roll(tile, 120, 1) * up + pltpu.roll(tile, 8, 1) * dn)


def key_docs(seg, j, blk):
    return jnp.broadcast_to(seg[j, 4:5, :], (blk, blk)).T


def attention_setup(qkv, gc, seg, kt, vt, gt, c_buf):
    blocks, _, blk, _ = qkv.shape
    for j in range(blocks):
        rows = pl.ds(j * blk, blk)
        kt[:, rows] = qkv[j, 1].astype(f32).T.astype(bf16)
        vt[:, rows] = qkv[j, 2].astype(f32).T.astype(bf16)
        gt[:, rows] = gc[j].astype(f32).T
    c_buf[...] = key_docs(seg, 0, blk)


def attention_block(h, i, qkv, seg, kt, vt, gt, p_buf, s_buf, acc, t_buf, c_buf):
    blocks, _, blk, lanes = qkv.shape
    half = lanes // 2
    lane = lax.broadcasted_iota(jnp.int32, (blk, lanes), 1) // half
    sub = lax.broadcasted_iota(jnp.int32, (lanes, blk), 0) // half
    causal = lax.broadcasted_iota(jnp.int32, (blk, blk), 0) <= lax.broadcasted_iota(jnp.int32, (blk, blk), 1)
    drow = seg[i, 4:5, :]
    own = pl.ds(pl.multiple_of(h * half, half), half)
    rest = pl.ds(pl.multiple_of((1 - h) * half, half), half)
    q_h = jnp.where(lane == h, qkv[i, 0].astype(f32) * 0.125, 0.0).astype(bf16)
    top = jnp.full((8, blk), masked_fill, f32)
    for j in range(i + 1):
        rows = pl.ds(j * blk, blk)
        s = nt(qkv[j, 1], q_h)
        seen = None
        if j == 0:
            seen = c_buf[...] == drow
        elif i == blocks - 1:
            seen = key_docs(seg, j, blk) == drow
        if j == i:
            seen = causal if seen is None else jnp.logical_and(causal, seen)
        if seen is not None:
            s = jnp.where(seen, s, masked_fill)
        s_buf[rows, :] = s
        top = jnp.maximum(top, jnp.max(s.reshape(blk // 8, 8, blk), axis=0))
    top = jnp.max(top, axis=0, keepdims=True)
    total = jnp.zeros((8, blk), f32)
    out = jnp.zeros((half, blk), f32)
    for j in range(i + 1):
        rows = pl.ds(j * blk, blk)
        p = jnp.exp(s_buf[rows, :] - top)
        s_buf[rows, :] = p
        total = total + jnp.sum(p.reshape(blk // 8, 8, blk), axis=0)
        rounded = p.astype(bf16)
        p_buf[j // 4, :, (j % 4) * blk : (j % 4 + 1) * blk] = rounded
        out = out + nn(vt[own, rows], rounded)
    inv = 1.0 / jnp.sum(total, axis=0, keepdims=True)
    out = out * inv
    t_buf[own, :] = out
    g_h = gt[own, i * blk : (i + 1) * blk]
    corr = jnp.sum(g_h * out, axis=0, keepdims=True) * inv
    gw = g_h * inv
    gw = jnp.concatenate([gw, gw], axis=0)
    gw_t = jnp.where(sub == h, gw, 0.0).astype(bf16)
    right = jnp.concatenate([q_h, jnp.where(sub == h, 0.0, gw).T.astype(bf16)], axis=0)
    dq = jnp.zeros((half, blk), f32)
    for j in range(i + 1):
        rows = pl.ds(j * blk, blk)
        ds = (s_buf[rows, :] * (nn(qkv[j, 2], gw_t) - corr)).astype(bf16)
        acc[rows, :] += nn(jnp.concatenate([ds, p_buf[j // 4, :, (j % 4) * blk : (j % 4 + 1) * blk]], axis=1), right)
        dq = dq + nn(kt[own, rows], ds)
    t_buf[rest, :] = dq * 0.125


SUM_AT = (5, 8, 11)


def kernel_m(
    n_f, n_c, n_y,
    x_hbm, dy_hbm, wq_hbm, wu_hbm, wd_hbm, wn_hbm, pk_hbm, pat_ref, vec_ref,
    out_ref, gx_ref, od_hbm, ou_hbm, on_hbm, oq_hbm, sum_ref,
    X, DY, WQ, WU, WD, WN, PK, N1, N2, XH, SQ, SG, ACT, GUP, PT, H2, GAIN, SMALL,
    CT, DQ, OR, HR, ROWS, GD, GU, GN, GQ, YD, YU, YN, YQ, ZD, ZU, ZN, ZQ, FD, FU, FN, FQ, UU, UQ, S1, R1, S2, R2, ES,
    AQ, AG, AS, KT, VT, GT, SB, DK, TB, CB, CX,
    loca, fsa, fra, vs, vr, asa, ara, fs, fr, as_, ar, ys, yr, zs, zr, gs, gr, hs, hr, own,
):
    me_f, me_c = lax.axis_index("fsdp"), lax.axis_index("ctx")
    rows, width = x_hbm.shape
    n_z, last = n_c // n_y, n_c // n_y - 1
    group = n_c // n_f
    qc, uc = WQ.shape[2], WU.shape[2]
    total, cut = n_f * rows, width // n_f

    bar = pltpu.get_barrier_semaphore()
    for d in range(1, n_f):
        pl.semaphore_signal(bar, inc=1, device_id=(flipped(me_f, d, n_f), me_c), device_id_type=MESH)
    for d in range(1, n_c):
        pl.semaphore_signal(bar, inc=1, device_id=(me_f, (me_c + d) % n_c), device_id_type=MESH)

    def cols(ref, i, n):
        return ref.at[:, pl.ds(pl.multiple_of(i * n, 128), n)]

    local = [
        pltpu.make_async_copy(x_hbm, X.at[me_f], loca.at[0]),
        pltpu.make_async_copy(pk_hbm, PK.at[me_f], loca.at[1]),
        pltpu.make_async_copy(cols(wq_hbm, me_f, qc), WQ.at[me_f], loca.at[2]),
        pltpu.make_async_copy(dy_hbm, DY.at[me_f], loca.at[3]),
        pltpu.make_async_copy(wn_hbm, WN, loca.at[4]),
        pltpu.make_async_copy(cols(wu_hbm, me_f, uc), WU.at[me_f], loca.at[5]),
        pltpu.make_async_copy(wd_hbm, WD, loca.at[6]),
    ]
    for cp in local:
        cp.start()
    pl.semaphore_wait(bar, n_f + n_c - 2)

    my_z, my_y = me_c // n_y, me_c % n_y
    other_y = 1 - my_y
    over_y = me_c + 1 - 2 * my_y
    over_z = me_c + n_y * (1 - 2 * (my_z % 2))
    quarter = WQ.shape[1] // 4

    def to_f(kind, d, src, dst, dest=None):
        return pltpu.make_async_remote_copy(
            src_ref=src, dst_ref=dst, send_sem=fsa.at[kind, d], recv_sem=fra.at[kind, d],
            device_id=(flipped(me_f, d, n_f) if dest is None else dest, me_c), device_id_type=MESH,
        )

    def part(ref, c):
        at = 2 * ((c // n_y) % 2) + c % n_y
        return ref.at[pl.ds(pl.multiple_of(at * quarter, 16), quarter)]

    def copy_of(kind, d):
        dest = flipped(me_f, d, n_f)
        if kind in (0, 1, 4):
            src, buf = ((x_hbm, X), (dy_hbm, DY), None, None, (pk_hbm, PK))[kind]
            return to_f(kind, d, src, buf.at[me_f])
        src, buf, n = ((wq_hbm, WQ, qc), (wu_hbm, WU, uc))[kind - 2]
        if d == 1:
            return to_f(kind, d, cols(src, dest, n), buf.at[me_f])
        return to_f(kind, d, cols(part(src, me_c), dest, n), part(buf.at[me_f], me_c))

    def arrival(kind, d):
        buf = (X, DY, WQ, WU, PK)[kind].at[flipped(me_f, d, n_f)]
        if kind in (2, 3) and d > 1:
            buf = part(buf, me_c)
        to_f(kind, d, buf, buf).wait_recv()

    def share(kind, d, way, mine=True):
        to, far = (over_y, over_z, over_z)[way], over_z + 1 - 2 * my_y
        which = (me_c, me_c, over_y)[way] if mine else (over_y, over_z, far)[way]
        buf = part((WQ, WU)[kind - 2].at[flipped(me_f, d, n_f)], which)
        return pltpu.make_async_remote_copy(
            src_ref=buf, dst_ref=buf, send_sem=vs.at[kind - 2, way, d], recv_sem=vr.at[kind - 2, way, d],
            device_id=(me_f, to), device_id_type=MESH,
        )

    def first_shares(kind):
        for d in range(2, n_f):
            arrival(kind, d)
            share(kind, d, 0).start()
            share(kind, d, 1).start()

    def next_shares(kind):
        for d in range(2, n_f):
            share(kind, d, 0, False).wait_recv()
            share(kind, d, 2).start()

    def weights(kind):
        arrival(kind, 1)
        for d in range(2, n_f):
            share(kind, d, 1, False).wait_recv()
            share(kind, d, 2, False).wait_recv()

    def forward(kind, d):
        buf = (X, DY)[kind].at[flipped(me_f, d, n_f)]
        return to_f(kind, d + 1, buf, buf, flipped(me_f, 1, n_f))

    direct = [1] + list(range(2, n_f, 2))
    for kind, to in ((4, range(1, n_f)), (2, (2, 3, 1)), (3, (2, 3, 1)), (0, direct), (1, direct)):
        for d in to:
            copy_of(kind, d).start()

    local[0].wait()
    local[1].wait()
    for d in range(1, n_f):
        arrival(4, d)
    for j in range(n_f):
        GAIN[0:4, j * (width // n_f) : (j + 1) * (width // n_f)] = PK[j, ROT : ROT + 4, :]
    g1, b1, g2, b2 = GAIN[0:1, :], GAIN[1:2, :], GAIN[2:3, :], GAIN[3:4, :]

    def norm_chunk(src):
        v = X[src].astype(f32)
        center = v - jnp.mean(v, axis=-1, keepdims=True)
        xhat = center * lax.rsqrt(jnp.mean(center * center, axis=-1, keepdims=True) + norm_eps)
        N1[src] = (xhat * g1 + b1).astype(bf16)
        N2[src] = (xhat * g2 + b2).astype(bf16)
        XH[src] = xhat.astype(bf16)

    lane_low = lax.broadcasted_iota(jnp.int32, (rows, 128), 1) < HD

    def to_heads(kind, k, src, dst):
        return pltpu.make_async_remote_copy(
            src_ref=src, dst_ref=dst, send_sem=asa.at[kind, k], recv_sem=ara.at[kind, k],
            device_id=(me_f, (me_c + k) % n_c), device_id_type=MESH,
        )

    def heads_arrival(kind):
        src, buf = ((SQ.at[0, 0], AQ), (SG.at[0, 0], AG), (PK.at[0, pl.ds(ROT, 8)], AS))[kind]
        pltpu.make_async_copy(src, buf.at[me_c], asa.at[kind, 0]).wait()
        for k in range(1, n_c):
            to_heads(kind, k, src, buf.at[(me_c - k + n_c) % n_c]).wait_recv()

    def to_c(kind, s, g, src, dst):
        dest = s * group + g
        k = (dest - me_c + n_c) % n_c

        @pl.when(k != 0)
        def _():
            to_heads(kind, k, src, dst).start()

        @pl.when(k == 0)
        def _():
            pltpu.make_async_copy(src, dst, asa.at[kind, 0]).start()

    def qkv_chunk(d, carry):
        s = flipped(me_f, d, n_f)
        table = tn(rotary_terms(PK[s]), pat_ref[...])
        mixed = nn(N1[s], WQ[...].reshape(width, qc)) + vec_ref[0:1, 0:qc]
        for g in range(group):
            t = [turn(mixed[:, g * 384 + i * 128 : g * 384 + (i + 1) * 128], table, i, 1.0) for i in range(3)]
            SQ[s, g, 0] = jnp.where(lane_low, t[0], t[1]).astype(bf16)
            SQ[s, g, 1] = jnp.where(lane_low, pltpu.roll(t[0], 64, 1), pltpu.roll(t[2], 64, 1)).astype(bf16)
            SQ[s, g, 2] = jnp.where(lane_low, t[1], t[2]).astype(bf16)
            to_c(0, s, g, SQ.at[s, g], AQ.at[me_c])
            to_c(2, s, g, PK.at[s, pl.ds(ROT, 8)], AS.at[me_c])
        return carry

    norm_chunk(me_f)
    first_shares(2)
    arrival(0, 1)
    norm_chunk(flipped(me_f, 1, n_f))
    first_shares(3)
    next_shares(2)
    next_shares(3)
    local[2].wait()
    weights(2)
    lax.fori_loop(0, 2, qkv_chunk, 0)
    for d in range(2, n_f):
        arrival(0, d)
        if d % 2 == 0:
            forward(0, d).start()
        norm_chunk(flipped(me_f, d, n_f))
        lax.fori_loop(d, d + 1, qkv_chunk, 0)
    local[3].wait()
    local[4].wait()
    for d in range(1, n_f):
        arrival(1, d)
        if d % 2 == 0:
            forward(1, d).start()

    def gc_chunk(d, carry):
        s = flipped(me_f, d, n_f)
        gc = nt(DY[s], WN[...])
        for g in range(group):
            SG[s, g] = gc[:, g * 128 : (g + 1) * 128].astype(bf16)
            to_c(1, s, g, SG.at[s, g], AG.at[me_c])
        return carry

    lax.fori_loop(0, n_f, gc_chunk, 0)
    local[5].wait()
    local[6].wait()
    weights(3)
    SMALL[...] = jnp.zeros_like(SMALL)

    def mlp_chunk(s, carry):
        up = nn(N2[s], WU[...].reshape(width, uc)) + vec_ref[1:2, 0:uc]
        cdf = 0.5 * (1.0 + lax.erf(up * (2.0 ** -0.5)))
        ACT[s] = (up * cdf).astype(bf16)
        slope = cdf + up * jnp.exp(-0.5 * up * up) * ((2.0 * np.pi) ** -0.5)
        gu = (nt(DY[s], WD[...]) * slope).astype(bf16)
        GUP[s] = gu
        SMALL[0:1, 0:uc] += jnp.sum(gu.astype(f32), axis=0, keepdims=True)
        SMALL[1:2, 0:width] += jnp.sum(DY[s].astype(f32), axis=0, keepdims=True)
        PT[s] = nn(ACT[s], WD[...]).astype(bf16)
        e = nt(GUP[s], WU[...].reshape(width, uc))
        SMALL[2:3, 0:width] += jnp.sum(e * XH[s].astype(f32), axis=0, keepdims=True)
        SMALL[3:4, 0:width] += jnp.sum(e, axis=0, keepdims=True)
        H2[s] = (e * g2).astype(bf16)
        return carry

    lax.fori_loop(0, n_f, mlp_chunk, 0)

    def down_grad(r, carry):
        at = pl.ds(pl.multiple_of(r * 256, 256), 256)
        per = 256 // (uc // n_c)
        res = tn(ACT[:, :, at].reshape(total, 256), DY[...].reshape(total, width)).astype(bf16)
        GD[pl.ds(r * per, per)] = res.reshape(per, uc // n_c, width)
        return carry

    def up_grad(r, carry):
        at = pl.ds(pl.multiple_of(r * 256, 256), 256)
        res = tn(N2[:, :, at].reshape(total, 256), GUP[...].reshape(total, uc)).astype(bf16)
        GU[:, r] = res.reshape(n_c, 256 // n_c, uc)
        return carry

    def remote(src, dst, ssem, rsem, dev):
        return pltpu.make_async_remote_copy(
            src_ref=src, dst_ref=dst, send_sem=ssem, recv_sem=rsem, device_id=dev, device_id_type=MESH)

    def result(pair, h, i):
        return GUP.at[2 * pair + h, :, pl.ds(pl.multiple_of(i * 128, 128), 128)]

    def back(pair, h, k, i):
        return remote(result(pair, h, i), (CT, DQ)[pair].at[me_c // group, me_c % group, h], as_.at[2 * pair + h, k],
                      ar.at[2 * pair + h, k], (me_f, (me_c + k) % n_c))

    def back_own(pair, h, i):
        return pltpu.make_async_copy(
            result(pair, h, i), (CT, DQ)[pair].at[me_c // group, me_c % group, h], as_.at[2 * pair + h, 0])

    def back_arrival(pair, h):
        back_own(pair, h, me_c).wait()
        for k in range(1, n_c):
            src = (me_c - k + n_c) % n_c
            buf = (CT, DQ)[pair].at[src // group, src % group, h]
            remote(buf, buf, as_.at[2 * pair + h, k], ar.at[2 * pair + h, k], (me_f, src)).wait_recv()

    def give(pair, h, t):
        i = (me_c + 1 + t) % n_c

        @pl.when(t < n_c - 1)
        def _():
            back(pair, h, t + 1, i).start()

        @pl.when(t == n_c - 1)
        def _():
            back_own(pair, h, i).start()

    G, YR, ZI, FP = (GD, GU, GN, GQ), (YD, YU, YN, YQ), (ZD, ZU, ZN, ZQ), (FD, FU, FN, FQ)
    UA, OUT = (None, UU, None, UQ), (od_hbm, ou_hbm, on_hbm, oq_hbm)
    low_half = 1 - my_z // (n_z // 2)

    def order(k):
        if k == last:
            return my_z
        down = last - k - (my_z - (last - k) + n_z) // n_z
        up = k + (k - my_z + n_z) // n_z
        return low_half * down + (1 - low_half) * up

    def toward(z):
        return (z - my_z + n_z) // n_z

    @pl.when(my_z == 0)
    def _():
        for buf in ZI:
            buf[1] = jnp.zeros(buf.shape[1:], bf16)

    @pl.when(my_z == last)
    def _():
        for buf in ZI:
            buf[0] = jnp.zeros(buf.shape[1:], bf16)

    def line_wait(item, way, z):
        @pl.when(jnp.logical_or(jnp.logical_and(way == 1, my_z > 0), jnp.logical_and(way == 0, my_z < last)))
        def _():
            line_copy(item, way, z, ZI[item].at[way, z]).wait_recv()

    def line_copy(item, way, z, src):
        return remote(src, ZI[item].at[way, z], zs.at[item, z], zr.at[item, way, z],
                      (me_f, (my_z + 2 * way - 1) * n_y + my_y))

    def y_send(item, z):
        src = G[item]
        return remote(src.at[z * n_y + other_y], YR[item].at[z], ys.at[item, z], yr.at[item, z],
                      (me_f, my_z * n_y + other_y))

    def y_start(item, k):
        y_send(item, order(k)).start()

    def y_sum(item, k):
        z = order(k)
        way = toward(z)
        y_send(item, z).wait_recv()
        line_wait(item, way, z)
        acc = YR[item][z].astype(f32) + G[item][z * n_y + my_y].astype(f32) + ZI[item][way, z].astype(f32)
        YR[item][z] = acc.astype(bf16)
        line_copy(item, way, z, YR[item].at[z]).start()

    def piece_total(item):
        y_send(item, my_z).wait_recv()
        for way in (0, 1):
            line_wait(item, way, my_z)
        acc = YR[item][my_z].astype(f32) + G[item][me_c].astype(f32)
        FP[item][...] = (acc + ZI[item][0, my_z].astype(f32) + ZI[item][1, my_z].astype(f32)).astype(bf16)

    def columns(item):
        n = FP[item].shape[2]
        return UA[item].at[:, pl.ds(pl.multiple_of(me_f * n, 128), n)]

    def f_send(item, d):
        dest = flipped(me_f, d, n_f)
        return remote(FP[item].at[dest], columns(item), fs.at[1 + item, d], fr.at[1 + item, d], (dest, me_c))

    def f_start(item):
        for d in range(1, n_f):
            f_send(item, d).start()
        columns(item)[...] = FP[item][me_f]

    def f_wait(item):
        for d in range(1, n_f):
            f_send(item, d).wait_recv()

    def ready(item):
        return FP[item] if UA[item] is None else UA[item]

    def g_send(item, z, step):
        src = ready(item) if z is None else OUT[item].at[z * n_y + my_y]
        at = my_z if z is None else z
        dst = OUT[item].at[at * n_y + my_y]
        return remote(src, dst, gs.at[item, (step + 1) // 2, at], gr.at[item, at],
                      (me_f, (my_z + step) * n_y + my_y))

    def h_send(item, z):
        src = ready(item) if z is None else OUT[item].at[z * n_y + my_y]
        at = my_z if z is None else z
        return remote(src, OUT[item].at[at * n_y + my_y], hs.at[item, at], hr.at[item, at],
                      (me_f, my_z * n_y + other_y))

    def spread(item):
        @pl.when(my_z < n_z - 1)
        def _():
            g_send(item, None, 1).start()

        @pl.when(my_z > 0)
        def _():
            g_send(item, None, -1).start()

        h_send(item, None).start()
        pltpu.make_async_copy(ready(item), OUT[item].at[me_c], own.at[item]).start()

    def pass_on(item, far):
        for step in (1, -1):
            z = my_z - step * far

            @pl.when(jnp.logical_and(z >= 0, z < n_z))
            def _(step=step, z=z):
                g_send(item, z, step).wait_recv()
                h_send(item, z).start()

                @pl.when(jnp.logical_and(my_z + step >= 0, my_z + step < n_z))
                def _():
                    g_send(item, z, step).start()

    def spread_wait(item):
        for step in (1, -1):

            @pl.when(jnp.logical_and(my_z + step >= 0, my_z + step < n_z))
            def _(step=step):
                g_send(item, None, step).wait_send()

            for far in range(1, n_z):
                z = my_z - step * far

                @pl.when(jnp.logical_and(jnp.logical_and(z >= 0, z < n_z),
                                         jnp.logical_and(my_z + step >= 0, my_z + step < n_z)))
                def _(step=step, z=z):
                    g_send(item, z, step).wait_send()

        for z in range(n_z):
            src = OUT[item].at[z * n_y + other_y]
            cp = remote(src, src, hs.at[item, z], hr.at[item, z], (me_f, my_z * n_y + other_y))
            cp.wait_send()
            cp.wait_recv()
        pltpu.make_async_copy(ready(item), OUT[item].at[me_c], own.at[item]).wait()

    lax.fori_loop(0, width // 256, down_grad, 0)
    for k in range(n_z):
        y_start(0, k)
    lax.fori_loop(0, width // 256, up_grad, 0)
    for k in range(n_z):
        y_start(1, k)

    at_end = jnp.logical_or(my_z == 0, my_z == last)
    between = jnp.logical_and(my_z > 0, my_z < last)

    @pl.when(at_end)
    def _():
        for k in range(last):
            y_sum(0, k)

    heads_arrival(0)
    heads_arrival(2)
    heads_arrival(1)
    attention_setup(AQ, AG, AS, KT, VT, GT, CB)

    def queries_of(i, h):
        def run():
            attention_block(h, i, AQ, AS, KT, VT, GT, ACT, SB, DK, TB, CB)
            GUP[h, :, i * 128 : (i + 1) * 128] = TB[...].T.astype(bf16)

        return run

    def one_head(h, carry):
        DK[...] = jnp.zeros_like(DK)

        def queries_step(t, inner):
            lax.switch((me_c + 1 + t) % n_c, [queries_of(i, h) for i in range(n_c)])
            give(0, h, t)
            for n, at in enumerate(SUM_AT):

                @pl.when(jnp.logical_and(h * n_c + t == at, between))
                def _(n=n):
                    y_sum(0, n)

            return inner

        lax.fori_loop(0, n_c, queries_step, 0)
        for i in range(n_c):
            GUP[2 + h, :, i * 128 : (i + 1) * 128] = DK[i * rows : (i + 1) * rows, :].astype(bf16)
        for t in range(n_c):
            give(1, h, t)
        return carry

    lax.fori_loop(0, 2, one_head, 0)
    piece_total(0)
    spread(0)

    @pl.when(at_end)
    def _():
        for k in range(last):
            y_sum(1, k)

    ROWS[...] = jnp.zeros_like(ROWS)
    for j in range(n_f):
        ROWS[0:1, j * cut : (j + 1) * cut] = PK[j, ROT : ROT + 1, :]
    ROWS[1:2, pl.ds(pl.multiple_of(me_f * cut, 128), cut)] = PK[me_f, ROT + 5 : ROT + 6, :]
    back_arrival(0, 0)
    back_arrival(0, 1)
    lane_low = lax.broadcasted_iota(jnp.int32, (rows, 128), 1) < HD

    def f_rows(kind, d, buf, land):
        dest = flipped(me_f, d, n_f)
        return remote(buf.at[dest], land.at[d - 1], fs.at[kind, d], fr.at[kind, d], (dest, me_c))

    def out_chunk(d, carry):
        s = flipped(me_f, d, n_f)
        for g in range(group):
            CX[s, :, g * 128 : (g + 1) * 128] = jnp.where(
                lane_low, CT[s, g, 0].astype(f32), CT[s, g, 1].astype(f32)).astype(bf16)
        PT[s] = (nn(CX[s], WN[...]) + PT[s].astype(f32) + ROWS[1:2, :]).astype(bf16)

        @pl.when(d != 0)
        def _():
            f_rows(0, d, PT, OR).start()

        return carry

    lax.fori_loop(0, n_f, out_chunk, 0)
    GN[...] = tn(CX[...].reshape(total, cut), DY[...].reshape(total, width)).astype(bf16).reshape(n_c, cut // n_c, width)
    for k in range(n_z):
        y_start(2, k)
    pass_on(0, 1)

    @pl.when(between)
    def _():
        y_sum(1, 0)

    back_arrival(1, 0)
    back_arrival(1, 1)
    ES[...] = jnp.zeros_like(ES)

    def mixed_chunk(d, carry):
        s = flipped(me_f, d, n_f)
        table = tn(rotary_terms(PK[s]), pat_ref[...])
        for g in range(group):
            c0, c1 = CT[s, g, 0].astype(f32), CT[s, g, 1].astype(f32)
            d0, d1 = DQ[s, g, 0].astype(f32), DQ[s, g, 1].astype(f32)
            t = [pltpu.roll(v, HD, 1) for v in (jnp.where(lane_low, d0, c0), jnp.where(lane_low, c1, d0), d1)]
            for i in range(3):
                lo = g * 384 + i * 128
                m = turn(t[i], table, i, -1.0).astype(bf16)
                N2[s, :, lo : lo + 128] = m
                ES[4:5, lo : lo + 128] += jnp.sum(m.astype(f32), axis=0, keepdims=True)
        e = nt(N2[s, :, 0:qc], WQ[...].reshape(width, qc))
        ES[0:1, :] += jnp.sum(e * XH[s].astype(f32), axis=0, keepdims=True)
        ES[1:2, :] += jnp.sum(e, axis=0, keepdims=True)
        H2[s] = (e * ROWS[0:1, :] + H2[s].astype(f32)).astype(bf16)

        @pl.when(d != 0)
        def _():
            f_rows(1, d, H2, HR).start()

        return carry

    lax.fori_loop(0, n_f, mixed_chunk, 0)
    tile = width // n_f

    def qkv_grad(r, carry):
        at = pl.ds(pl.multiple_of(r * tile, tile), tile)
        res = tn(N1[:, :, at].reshape(total, tile), N2[:, :, 0:qc].reshape(total, qc)).astype(bf16)
        GQ[:, r] = res.reshape(n_c, tile // n_c, qc)
        return carry

    lax.fori_loop(0, n_f, qkv_grad, 0)
    for k in range(n_z):
        y_start(3, k)

    for j in range(n_f):
        S1[j, 0:2, :] = ES[0:2, j * tile : (j + 1) * tile]
        S1[j, 2:4, :] = SMALL[2:4, j * tile : (j + 1) * tile]
        S1[j, 4:8, :] = jnp.zeros((4, tile), f32)
    for d in range(1, n_f):
        f_rows(3, d, S1, R1).start()

    @pl.when(between)
    def _():
        y_sum(1, 1)
        y_sum(1, 2)

    for k in range(last):
        y_sum(2, k)
    pass_on(0, 2)
    piece_total(1)
    f_start(1)
    pass_on(0, 3)
    for k in range(last):
        y_sum(3, k)
    piece_total(2)
    spread(2)
    f_wait(1)
    spread(1)

    for d in range(1, n_f):
        f_rows(3, d, S1, R1).wait_recv()
    S2[...] = jnp.zeros_like(S2)
    S2[0:1, 0:qc] = ES[4:5, 0:qc]
    S2[1:2, :] = SMALL[0:1, :]
    S2[2:3, 0:tile] = SMALL[1:2, pl.ds(pl.multiple_of(me_f * tile, tile), tile)]
    vec = S1[me_f, 0:4, :]
    for d in range(1, n_f):
        vec = vec + R1[d - 1, 0:4, :]
    S2[3:7, 0:tile] = vec

    def s2_send(k):
        dest = (me_c + k) % n_c
        return remote(S2, R2.at[k], as_.at[4, k], ar.at[4, k], (me_f, dest))

    for k in range(1, n_c):
        s2_send(k).start()

    piece_total(3)
    f_start(3)
    pass_on(1, 1)
    pass_on(2, 1)
    f_wait(3)
    spread(3)
    pass_on(1, 2)
    pass_on(2, 2)
    for d in range(1, n_f):
        f_rows(0, d, PT, OR).wait_recv()
    v = X[me_f].astype(f32)
    acc = v + PT[me_f].astype(f32)
    for d in range(1, n_f):
        acc = acc + OR[d - 1].astype(f32)
    out_ref[...] = acc.astype(bf16)

    pass_on(3, 1)
    pass_on(1, 3)
    pass_on(2, 3)
    for d in range(1, n_f):
        f_rows(1, d, H2, HR).wait_recv()
    h = H2[me_f].astype(f32)
    for d in range(1, n_f):
        h = h + HR[d - 1].astype(f32)
    center = v - jnp.mean(v, axis=-1, keepdims=True)
    rstd = lax.rsqrt(jnp.mean(center * center, axis=-1, keepdims=True) + norm_eps)
    xhat = center * rstd
    grad = rstd * (h - jnp.mean(h, axis=-1, keepdims=True) - xhat * jnp.mean(h * xhat, axis=-1, keepdims=True))
    gx_ref[...] = (DY[me_f].astype(f32) + grad).astype(bf16)
    pass_on(3, 2)
    pass_on(3, 3)
    tot = S2[...]
    for k in range(1, n_c):
        s2_send(k).wait_recv()
        tot = tot + R2[k]
    sum_ref[...] = tot

    for kind in range(5):
        for d in range(1, n_f):
            if kind < 2 and d % 2 == 1 and d > 1:
                forward(kind, d - 1).wait_send()
            else:
                copy_of(kind, d).wait_send()
            if kind in (2, 3) and d > 1:
                for way in range(3):
                    share(kind, d, way).wait_send()
    for kind, src in ((0, SQ.at[0, 0]), (1, SG.at[0, 0]), (2, PK.at[0, pl.ds(ROT, 8)])):
        for k in range(1, n_c):
            to_heads(kind, k, src, src).wait_send()
    for k in range(1, n_c):
        for kind in range(4):
            back(kind // 2, kind % 2, k, (me_c + k) % n_c).wait_send()
        s2_send(k).wait_send()
    for d in range(1, n_f):
        f_rows(0, d, PT, OR).wait_send()
        f_rows(1, d, H2, HR).wait_send()
        f_rows(3, d, S1, R1).wait_send()
        f_send(1, d).wait_send()
        f_send(3, d).wait_send()
    for item in range(4):
        for z in range(n_z):
            y_send(item, z).wait_send()

            @pl.when(my_z != z)
            def _(item=item, z=z):
                line_copy(item, toward(z), z, YR[item].at[z]).wait_send()

        spread_wait(item)


def call_m(n_f, n_c, n_y, x, dy, wq, wu, wd, wn, pk, vectors):
    rows, width = x.shape
    qc, uc = wq.shape[1] // n_f, wu.shape[1] // n_f
    n_z, group, cut, n = n_c // n_y, n_c // n_f, width // n_f, n_c * rows
    S, V, D = jax.ShapeDtypeStruct, pltpu.VMEM, pltpu.SemaphoreType.DMA
    pat = jnp.asarray(rotary_pattern(), bf16)
    shapes = [(uc // n_c, width), (n_f, cut // n_c, uc), (cut // n_c, width), (n_f, cut // n_c, qc)]
    wides = [shapes[0], (cut // n_c, n_f * uc), shapes[2], (cut // n_c, n_f * qc)]
    act = V((n_f, rows, width), bf16)
    scratch = [
        act, act, V((n_f, cut, qc), bf16), V((n_f, cut, uc), bf16), V((uc, width), bf16), V((cut, width), bf16),
        V((n_f,) + pk.shape, f32), act, act, act, V((n_f, group, 3, rows, 128), bf16), V((n_f, group, rows, 128), bf16),
        V((n_f, rows, uc), bf16), V((n_f, rows, uc), bf16), act, act, V((8, width), f32), V((8, max(uc, width)), f32),
    ]
    scratch += [
        V((n_f, group, 2, rows, 128), bf16), V((n_f, group, 2, rows, 128), bf16),
        V((n_f - 1, rows, width), bf16), V((n_f - 1, rows, width), bf16), V((8, width), f32),
    ]
    scratch += [V((n_c,) + s, bf16) for s in shapes]
    scratch += [V((n_z,) + s, bf16) for s in shapes]
    scratch += [V((2, n_z) + s, bf16) for s in shapes]
    scratch += [V(s, bf16) for s in shapes] + [V(wides[1], bf16), V(wides[3], bf16)]
    scratch += [V((n_f, 8, cut), f32), V((n_f - 1, 8, cut), f32), V((8, uc), f32), V((n_c, 8, uc), f32), V((8, width), f32)]
    scratch += [
        V((n_c, 3, rows, 128), bf16), V((n_c, rows, 128), bf16), V((n_c, 8, rows), f32), V((128, n), bf16), V((128, n), bf16),
        V((128, n), f32), V((n, rows), f32), V((n, 128), f32), V((128, rows), f32), V((rows, rows), f32),
        V((n_f, rows, cut), bf16),
    ]
    scratch += [
        D((7,)), D((5, n_f)), D((5, n_f)), D((2, 3, n_f)), D((2, 3, n_f)), D((3, n_c)), D((3, n_c)),
        D((5, n_f)), D((5, n_f)), D((5, n_c)), D((5, n_c)),
        D((4, n_z)), D((4, n_z)), D((4, n_z)), D((4, 2, n_z)), D((4, 2, n_z)), D((4, n_z)), D((4, n_z)), D((4, n_z)), D((4,)),
    ]
    return pl.pallas_call(
        functools.partial(kernel_m, n_f, n_c, n_y),
        out_shape=(S((rows, width), bf16), S((rows, width), bf16))
        + tuple(S((n_c,) + s, bf16) for s in wides) + (S((8, uc), f32),),
        in_specs=[hbm] * 7 + [vmem] * 2,
        out_specs=(vmem, vmem) + (hbm,) * 4 + (vmem,),
        scratch_shapes=scratch,
        compiler_params=pltpu.CompilerParams(collective_id=0, has_side_effects=True, vmem_limit_bytes=63 * 2**20),
        name="layer",
    )(x, dy, wq, wu, wd, wn, pk, pat, vectors)


def kernel_d(od, ou, on, oq, out, gx, vec, fd, fu, fn, fq, o1, o2, bq, b1, bu, n1g, n1b, n2g, n2b):
    for src, dst in ((od, fd), (ou, fu), (on, fn), (oq, fq)):
        dst[...] = src[0].astype(f32)
    o1[...] = out[...]
    o2[...] = gx[...]

    @pl.when(pl.program_id(0) == 0)
    def _():
        for ref, row in ((bq, 0), (bu, 1), (b1, 2), (n1g, 3), (n1b, 4), (n2g, 5), (n2b, 6)):
            ref[...] = vec[row, 0 : ref.shape[0]]


def call_d(od, ou, on, oq, out, gx, vec, qc):
    n_c, rows, cut = od.shape[0], out.shape[0], on.shape[0] * on.shape[1]
    S = jax.ShapeDtypeStruct

    def whole(n):
        return pl.BlockSpec((n,), lambda i: (0,))

    def block(a):
        return pl.BlockSpec((1,) + a.shape[1:], lambda i: (i, 0, 0))

    def flat(a):
        return pl.BlockSpec(a.shape[1:], lambda i: (i, 0))

    strip = pl.BlockSpec((rows // n_c, out.shape[1]), lambda i: (i, 0))
    grads = (od, ou, on, oq)
    sizes = (qc, cut, vec.shape[1], cut, cut, cut, cut)
    return pl.pallas_call(
        kernel_d,
        grid=(n_c,),
        out_shape=tuple(S((n_c * a.shape[1], a.shape[2]), f32) for a in grads)
        + (S(out.shape, bf16), S(out.shape, bf16)) + tuple(S((n,), f32) for n in sizes),
        in_specs=[block(a) for a in grads] + [strip, strip, pl.BlockSpec(vec.shape, lambda i: (0, 0))],
        out_specs=tuple(flat(a) for a in grads) + (strip, strip) + tuple(whole(n) for n in sizes),
        compiler_params=pltpu.CompilerParams(vmem_limit_bytes=62 * 2**20),
        name="widen",
    )(od, ou, on, oq, out, gx, vec)


def low(v):
    return v.astype(bf16)


def rotate_back(grad_part, cosine_table, sine_table):
    half_rot = ROT // 2
    g = grad_part[..., :ROT]
    b = g * sine_table[:, None, :]
    turned = jnp.concatenate([b[..., half_rot:], -b[..., :half_rot]], axis=-1)
    return jnp.concatenate([g * cosine_table[:, None, :] + turned, grad_part[..., ROT:]], axis=-1)


def body(
    tokens, segments, positions, cotangent, qkv_weight, qkv_bias, dense_weight, dense_bias,
    up_weight, up_bias, down_weight, down_bias, norm1_gain, norm1_bias, norm2_gain, norm2_bias,
):
    n_f, n_c = lax.axis_size("fsdp"), lax.axis_size("ctx")
    n_y = 2
    pk, vectors = call_p(positions, segments, norm1_gain, norm1_bias, norm2_gain, norm2_bias,
                         dense_bias, down_bias, qkv_bias, up_bias)
    out, gx, od, ou, on, oq, vec = call_m(
        n_f, n_c, n_y, tokens, cotangent, qkv_weight, up_weight, down_weight, dense_weight, pk, vectors)
    gd, gu, gn, gq, out, gx, bq, b1, bu, n1g, n1b, n2g, n2b = call_d(
        od, ou, on, oq, out, gx, vec, qkv_bias.shape[0])
    return out, gx, gq, bq, gn, b1, gu, bu, gd, b1, n1g, n1b, n2g, n2b


def rotary_tables(places):
    half_rot = ROT // 2
    inverse = 10000.0 ** (-2.0 * jnp.arange(half_rot, dtype=jnp.float32) / ROT)
    angles = places.astype(jnp.float32)[:, None] * inverse[None, :]
    angles = jnp.concatenate([angles, angles], axis=1)
    return (jnp.cos(angles), jnp.sin(angles))


def rotate(head_part, cosine_table, sine_table):
    half_rot = ROT // 2
    rotated_part = head_part[..., :ROT]
    turned = jnp.concatenate([-rotated_part[..., half_rot:], rotated_part[..., :half_rot]], axis=-1)
    rotated_part = rotated_part * cosine_table[:, None, :] + turned * sine_table[:, None, :]
    return jnp.concatenate([rotated_part, head_part[..., ROT:]], axis=-1)


def attention_pair(q, k, v, gc, doc):
    length = q.shape[0]
    place = jnp.arange(length, dtype=jnp.int32)
    visible = (place[None, :] <= place[:, None]) & (doc[None, :] == doc[:, None])
    scores = nt(q, k) * (1.0 / math.sqrt(HD))
    row_max = jnp.max(jnp.where(visible, scores, masked_fill), axis=-1, keepdims=True)
    terms = jnp.where(visible, jnp.exp(jnp.where(visible, scores - row_max, 0.0)), 0.0)
    total = jnp.sum(terms, axis=-1, keepdims=True)
    context = nn(low(terms), v) / total
    correction = jnp.sum(gc * context, axis=-1, keepdims=True) / total
    gw = low(gc / total)
    gv = tn(low(terms), gw)
    gs = low(terms * (nt(gw, v) - correction))
    gq = nn(gs, k) * (1.0 / math.sqrt(HD))
    gk = tn(gs, q) * (1.0 / math.sqrt(HD))
    return context, gq, gk, gv


def plain_body(
    tokens, segments, positions, cotangent, qkv_weight, qkv_bias, dense_weight, dense_bias,
    up_weight, up_bias, down_weight, down_bias, norm1_gain, norm1_bias, norm2_gain, norm2_bias,
):
    f32 = jnp.float32
    n_f, n_c = lax.axis_size("fsdp"), lax.axis_size("ctx")
    rows, width = tokens.shape
    heads = width // HD
    pairs = heads // n_c
    group = n_c // n_f
    me_c = lax.axis_index("ctx")
    me_f = lax.axis_index("fsdp")

    x = lax.all_gather(tokens, "fsdp", axis=0, tiled=True).astype(f32)
    dy = lax.all_gather(cotangent, "fsdp", axis=0, tiled=True)
    pos = lax.all_gather(positions, "fsdp", axis=0, tiled=True)
    docs = lax.all_gather(segments, ("fsdp", "ctx"), axis=0, tiled=True)
    w_qkv = lax.all_to_all(qkv_weight, "fsdp", 1, 0, tiled=True)
    w_up = lax.all_to_all(up_weight, "fsdp", 1, 0, tiled=True)
    norms = lax.all_gather(
        jnp.stack([norm1_gain, norm1_bias, norm2_gain, norm2_bias]), "fsdp", axis=1, tiled=True
    ).astype(f32)

    center = x - jnp.mean(x, axis=-1, keepdims=True)
    rstd = lax.rsqrt(jnp.mean(center * center, axis=-1, keepdims=True) + norm_eps)
    xhat = center * rstd
    normed_one = low(xhat * norms[0] + norms[1])
    normed_two = low(xhat * norms[2] + norms[3])

    mixed = nn(normed_one, w_qkv) + qkv_bias.astype(f32)
    total_rows = x.shape[0]
    cos, sin = rotary_tables(pos)
    mixed = mixed.reshape(total_rows, heads // n_f, 3, HD)
    mixed = jnp.stack(
        [rotate(mixed[:, :, 0], cos, sin), rotate(mixed[:, :, 1], cos, sin), mixed[:, :, 2]], axis=2
    )

    def to_heads(a, cols):
        a = a.reshape(n_f, rows, group, cols).transpose(0, 2, 1, 3).reshape(n_c, rows, cols)
        return lax.all_to_all(a, "ctx", 0, 0, tiled=True).reshape(n_c * rows, cols)

    def to_tokens(a, cols):
        a = lax.all_to_all(a.reshape(n_c, rows, cols), "ctx", 0, 0, tiled=True)
        return a.reshape(n_f, group, rows, cols).transpose(0, 2, 1, 3).reshape(total_rows, group * cols)

    qkv = to_heads(low(mixed).reshape(total_rows, -1), pairs * 3 * HD).reshape(-1, pairs, 3, HD)
    grad_context = nt(dy, dense_weight)
    gc = to_heads(low(grad_context), pairs * HD).reshape(-1, pairs, HD).astype(f32)
    seq_doc = lax.dynamic_slice_in_dim(docs, (me_c // group) * (n_c * rows), n_c * rows, 0)

    results = [
        attention_pair(qkv[:, i, 0], qkv[:, i, 1], qkv[:, i, 2], gc[:, i], seq_doc) for i in range(pairs)
    ]
    context = to_tokens(low(jnp.concatenate([r[0] for r in results], axis=1)), pairs * HD)
    grads = jnp.stack([jnp.stack(r[1:], axis=1) for r in results], axis=1)
    grads = to_tokens(low(grads).reshape(n_c * rows, -1), pairs * 3 * HD).astype(f32)
    grads = grads.reshape(total_rows, heads // n_f, 3, HD)
    grad_mixed = low(
        jnp.stack(
            [rotate_back(grads[:, :, 0], cos, sin), rotate_back(grads[:, :, 1], cos, sin), grads[:, :, 2]],
            axis=2,
        )
    ).reshape(total_rows, -1)

    up = nn(normed_two, w_up) + up_bias.astype(f32)
    active, pull = jax.vjp(lambda v: jax.nn.gelu(v, approximate=False), up)
    active = low(active)
    grad_up = low(pull(nt(dy, down_weight))[0])
    g_up_w = tn(normed_two, grad_up)
    g_up_b = jnp.sum(grad_up.astype(f32), axis=0)
    g_down_w = tn(active, dy)
    e_two = nt(grad_up, w_up)

    part = nn(context, dense_weight) + nn(active, down_weight)
    bias = lax.dynamic_update_slice_in_dim(
        jnp.zeros((width,), f32), dense_bias.astype(f32) + down_bias.astype(f32), me_f * (width // n_f), 0
    )
    part = low(part + bias)
    out = lax.psum_scatter(part, "fsdp", scatter_dimension=0, tiled=True).astype(f32)
    layer_out = low(tokens.astype(f32) + out)

    g_dense_w = tn(context, dy)
    g_qkv_w = tn(normed_one, grad_mixed)
    g_qkv_b = jnp.sum(grad_mixed.astype(f32), axis=0)
    e_one = nt(grad_mixed, w_qkv)
    h = low(e_one * norms[0] + e_two * norms[2])
    h = lax.psum_scatter(h, "fsdp", scatter_dimension=0, tiled=True).astype(f32)
    own_xhat = lax.dynamic_slice_in_dim(xhat, me_f * rows, rows, 0)
    own_rstd = lax.dynamic_slice_in_dim(rstd, me_f * rows, rows, 0)
    grad_in = own_rstd * (
        h - jnp.mean(h, axis=-1, keepdims=True) - own_xhat * jnp.mean(h * own_xhat, axis=-1, keepdims=True)
    )
    grad_tokens = low(cotangent.astype(f32) + grad_in)
    vecs = jnp.stack(
        [jnp.sum(e_one * xhat, 0), jnp.sum(e_one, 0), jnp.sum(e_two * xhat, 0), jnp.sum(e_two, 0)]
    )
    vecs = lax.psum(lax.psum_scatter(vecs, "fsdp", scatter_dimension=1, tiled=True), "ctx")
    dy_sum = jnp.sum(cotangent.astype(f32), axis=0)
    dy_sum = lax.psum(lax.psum_scatter(dy_sum, "fsdp", scatter_dimension=0, tiled=True), "ctx")
    g_qkv_b = lax.psum(g_qkv_b, "ctx")
    g_up_b = lax.psum(g_up_b, "ctx")

    def reduced(g, columns):
        if columns:
            g = lax.psum_scatter(low(g).reshape(n_f, -1, g.shape[1]), "ctx", scatter_dimension=1, tiled=True)
            g = lax.all_to_all(g, "fsdp", 0, 0, tiled=True)
            g = g.transpose(1, 0, 2).reshape(g.shape[1], -1)
            return lax.all_gather(g, "ctx", axis=0, tiled=True).astype(f32)
        g = lax.psum_scatter(low(g), "ctx", scatter_dimension=0, tiled=True)
        return lax.all_gather(g, "ctx", axis=0, tiled=True).astype(f32)

    return (
        layer_out, grad_tokens,
        reduced(g_qkv_w, True), g_qkv_b, reduced(g_dense_w, False), dy_sum,
        reduced(g_up_w, True), g_up_b, reduced(g_down_w, False), dy_sum,
        vecs[0], vecs[1], vecs[2], vecs[3],
    )


def solution(mesh):
    n_f, n_c = mesh.shape["fsdp"], mesh.shape["ctx"]
    fits = n_c % n_f == 0 and n_c == 8 and n_f == 4
    row, flat, w, b = P(("fsdp", "ctx"), None), P(("fsdp", "ctx")), P("fsdp", None), P("fsdp")
    return jax.shard_map(
        body if fits else plain_body,
        mesh=mesh,
        in_specs=(row, flat, flat, row, w, b, w, b, w, b, w, b, b, b, b, b),
        out_specs=(row, row, w, b, w, b, w, b, w, b, b, b, b, b),
        check_vma=False,
    )
```

time: 1080 us -> 261 us (0.24)
  waiting for transfers between devices: 545 us -> 0 us
  Pallas kernels: 0 us -> 259 us
  matrix products: 174 us -> 0 us
  blocking collectives: 97 us -> 0 us
  starting transfers between devices: 96.6 us -> 0 us
  other arithmetic: 77 us -> 0 us
  local copies, waits for them, and re-layouts: 67.2 us -> 1.24 us
  between operations: 16.9 us -> 0.67 us
    pallas_call x0 -> x3, Pallas kernels: none -> 259 us  [the longest x1 248 us: call_m(): pl.pallas_call(functools.partial(kernel_m, n_f, n_c, n_y), out_shape=(S((...]
    ppermute x30 -> x0, waiting for transfers between devices: 178 us -> none  [the longest x14 100 us: passed_along(): return lax.ppermute(block, axis, route)]
    dot_general x60 -> x0, matrix products: 174 us -> none  [the longest x4 32.5 us: right_product(): lax.dot_general(left_arg, right_arg, (((1,), (1,)), ((), ())), preferred_...]
    all_gather x6 -> x0, waiting for transfers between devices: 163 us -> none  [the longest x1 62.5 us: body(): key_piece = lax.all_gather(keys_own, 'ctx', axis=0, tiled=True)]
    psum x1 -> x0, waiting for transfers between devices: 144 us -> none  [body(): lax.psum(part_qkv_w.astype(jnp.bfloat16), 'ctx').astype(jnp.float32)]
    ppermute x30 -> x0, starting transfers between devices: 95.4 us -> none  [the longest x14 73.1 us: passed_along(): return lax.ppermute(block, axis, route)]
    all_gather x9 -> x0, blocking collectives: 62.7 us -> none  [the longest x1 20.7 us: body(): doc_all = lax.all_gather(segments, 'ctx', axis=0, tiled=True)]
    reduce_scatter x4 -> x0, waiting for transfers between devices: 58.6 us -> none  [the longest x1 58.5 us: body(): lax.psum_scatter(grad_qkv_w.astype(jnp.bfloat16), 'fsdp', scatter_dimensi...]
  transfers between devices with their start and end apart: 41 -> 0, of which waited for: 34 -> 0; matrix products, arithmetic and copies ran while one was open for 28% -> 0% of each run, Pallas kernels for 0% -> 0%
where the time goes in v1:
time: 261 us
  Pallas kernels  259 us (99%)
    pallas_call x1, Pallas kernels, call_m(): pl.pallas_call(functools.partial(kernel_m, n_f, n_c, n_y), out_shape=(S((...  248 us
    pallas_call x1, Pallas kernels, call_d(): pl.pallas_call(kernel_d, grid=(n_c,), out_shape=tuple((S((n_c * a.shape[1...  9.5 us

profile of v1, /device:TPU:0, one launch (start us, length us, event | category | flops | bytes accessed | tf_op | source)
XLA Modules:
  0.0 260.8 jit_solution(4052305151066801985)
XLA Ops:
  0.6 1.5 pack.1
  2.2 247.9 %layer.1 = (bf16[256,1024]{1,0:T(8,128)(2,1)}, bf16[256,1024]{1,0:T(8,128)(2,1)}, bf16[8,128,1024]{2,1,0:T(8,128)(2,1)}, bf16[8,32,4096]{2,1,0:T(8,128)(2,1)}, b...) custom-call(bf16[256,1024]{1,0:T(8,128)(2,1)} %x_hbm.1, bf16[256,1024]{1,0:T(8,128)(2,1)} %dy_hbm.1, ...), custom_call_target="tpu_custom_call" | custom-call | tf_op jit(solution)/shard_map/layer/pallas_call | solution.py:853
  250.0 9.5 %widen.1 = (f32[1024,1024]{1,0:T(8,128)}, f32[256,4096]{1,0:T(8,128)}, f32[256,1024]{1,0:T(8,128)}, f32[256,3072]{1,0:T(8,128)}, bf16[256,1024]{1,0:T(8,128)(2,1...) custom-call(bf16[8,128,1024]{2,1,0:T(8,128)(2,1)} %get-tuple-element, ...), custom_call_target="tpu_custom_call" | custom-call | tf_op jit(solution)/shard_map/widen/pallas_call | solution.py:893
  259.5 1.2 copy.32

commit v2 on v1

--- a/solution.py
+++ b/solution.py
@@ -171,7 +171,7 @@
     t_buf[rest, :] = dq * 0.125
 
 
-SUM_AT = (5, 8, 11)
+SUMS_IN = ((1, 0, 1, (0, 1, 2)), (4, 1, 0, (0,)), (6, 1, 1, (0,)), (9, 1, 0, (1, 2)), (12, 1, 1, (1, 2)))
 
 
 def kernel_m(
@@ -350,12 +350,39 @@
             forward(0, d).start()
         norm_chunk(flipped(me_f, d, n_f))
         lax.fori_loop(d, d + 1, qkv_chunk, 0)
+    local[5].wait()
+    local[6].wait()
+    weights(3)
+    SMALL[...] = jnp.zeros_like(SMALL)
+
+    def mlp_forward(s, carry):
+        up = nn(N2[s], WU[...].reshape(width, uc)) + vec_ref[1:2, 0:uc]
+        cdf = 0.5 * (1.0 + lax.erf(up * (2.0 ** -0.5)))
+        ACT[s] = (up * cdf).astype(bf16)
+        GUP[s] = (cdf + up * jnp.exp(-0.5 * up * up) * ((2.0 * np.pi) ** -0.5)).astype(bf16)
+        PT[s] = nn(ACT[s], WD[...]).astype(bf16)
+        return carry
+
+    def mlp_backward(s, carry):
+        gu = (nt(DY[s], WD[...]) * GUP[s].astype(f32)).astype(bf16)
+        GUP[s] = gu
+        SMALL[0:1, 0:uc] += jnp.sum(gu.astype(f32), axis=0, keepdims=True)
+        SMALL[1:2, 0:width] += jnp.sum(DY[s].astype(f32), axis=0, keepdims=True)
+        e = nt(GUP[s], WU[...].reshape(width, uc))
+        SMALL[2:3, 0:width] += jnp.sum(e * XH[s].astype(f32), axis=0, keepdims=True)
+        SMALL[3:4, 0:width] += jnp.sum(e, axis=0, keepdims=True)
+        H2[s] = (e * g2).astype(bf16)
+        return carry
+
+    lax.fori_loop(0, n_f // 2, mlp_forward, 0)
+    for d in range(2, n_f, 2):
+        arrival(1, d)
+        forward(1, d).start()
+    lax.fori_loop(n_f // 2, n_f, mlp_forward, 0)
     local[3].wait()
     local[4].wait()
-    for d in range(1, n_f):
+    for d in range(1, n_f, 2):
         arrival(1, d)
-        if d % 2 == 0:
-            forward(1, d).start()
 
     def gc_chunk(d, carry):
         s = flipped(me_f, d, n_f)
@@ -366,40 +393,23 @@
         return carry
 
     lax.fori_loop(0, n_f, gc_chunk, 0)
-    local[5].wait()
-    local[6].wait()
-    weights(3)
-    SMALL[...] = jnp.zeros_like(SMALL)
-
-    def mlp_chunk(s, carry):
-        up = nn(N2[s], WU[...].reshape(width, uc)) + vec_ref[1:2, 0:uc]
-        cdf = 0.5 * (1.0 + lax.erf(up * (2.0 ** -0.5)))
-        ACT[s] = (up * cdf).astype(bf16)
-        slope = cdf + up * jnp.exp(-0.5 * up * up) * ((2.0 * np.pi) ** -0.5)
-        gu = (nt(DY[s], WD[...]) * slope).astype(bf16)
-        GUP[s] = gu
-        SMALL[0:1, 0:uc] += jnp.sum(gu.astype(f32), axis=0, keepdims=True)
-        SMALL[1:2, 0:width] += jnp.sum(DY[s].astype(f32), axis=0, keepdims=True)
-        PT[s] = nn(ACT[s], WD[...]).astype(bf16)
-        e = nt(GUP[s], WU[...].reshape(width, uc))
-        SMALL[2:3, 0:width] += jnp.sum(e * XH[s].astype(f32), axis=0, keepdims=True)
-        SMALL[3:4, 0:width] += jnp.sum(e, axis=0, keepdims=True)
-        H2[s] = (e * g2).astype(bf16)
-        return carry
-
-    lax.fori_loop(0, n_f, mlp_chunk, 0)
+
 
     def down_grad(r, carry):
         at = pl.ds(pl.multiple_of(r * 256, 256), 256)
         per = 256 // (uc // n_c)
         res = tn(ACT[:, :, at].reshape(total, 256), DY[...].reshape(total, width)).astype(bf16)
-        GD[pl.ds(r * per, per)] = res.reshape(per, uc // n_c, width)
+        res = res.reshape(per, 2, uc // n_c // 2, width)
+        for i in range(2):
+            GD[i, pl.ds(r * per, per)] = res[:, i]
         return carry
 
     def up_grad(r, carry):
         at = pl.ds(pl.multiple_of(r * 256, 256), 256)
         res = tn(N2[:, :, at].reshape(total, 256), GUP[...].reshape(total, uc)).astype(bf16)
-        GU[:, r] = res.reshape(n_c, 256 // n_c, uc)
+        res = res.reshape(n_c, 2, 256 // n_c // 2, uc)
+        for i in range(2):
+            GU[i, :, r] = res[:, i]
         return carry
 
     def remote(src, dst, ssem, rsem, dev):
@@ -435,8 +445,19 @@
         def _():
             back_own(pair, h, i).start()
 
-    G, YR, ZI, FP = (GD, GU, GN, GQ), (YD, YU, YN, YQ), (ZD, ZU, ZN, ZQ), (FD, FU, FN, FQ)
-    UA, OUT = (None, UU, None, UQ), (od_hbm, ou_hbm, on_hbm, oq_hbm)
+    def items(d, u, n, q):
+        return [d.at[0], d.at[1], u.at[0], u.at[1], n, q.at[0], q.at[1]]
+
+    G, YR, ZI = items(GD, GU, GN, GQ), items(YD, YU, YN, YQ), items(ZD, ZU, ZN, ZQ)
+    FP = items(FD, FU, FN, FQ)
+    UA = [None, None, UU.at[0], UU.at[1], None, UQ.at[0], UQ.at[1]]
+    DOWN, UP, DENSE, QKV = (0, 1), (2, 3), (4,), (5, 6)
+
+    def out_at(item, c):
+        if item in DENSE:
+            return on_hbm.at[c]
+        return (od_hbm if item in DOWN else ou_hbm if item in UP else oq_hbm).at[c, item - (0, 0, 2, 2, 4, 5, 5)[item]]
+
     low_half = 1 - my_z // (n_z // 2)
 
     def order(k):
@@ -451,13 +472,15 @@
 
     @pl.when(my_z == 0)
     def _():
-        for buf in ZI:
-            buf[1] = jnp.zeros(buf.shape[1:], bf16)
+        for buf in (ZD, ZU, ZQ):
+            buf[:, 1] = jnp.zeros(buf.shape[:1] + buf.shape[2:], bf16)
+        ZN[1] = jnp.zeros(ZN.shape[1:], bf16)
 
     @pl.when(my_z == last)
     def _():
-        for buf in ZI:
-            buf[0] = jnp.zeros(buf.shape[1:], bf16)
+        for buf in (ZD, ZU, ZQ):
+            buf[:, 0] = jnp.zeros(buf.shape[:1] + buf.shape[2:], bf16)
+        ZN[0] = jnp.zeros(ZN.shape[1:], bf16)
 
     def line_wait(item, way, z):
         @pl.when(jnp.logical_or(jnp.logical_and(way == 1, my_z > 0), jnp.logical_and(way == 0, my_z < last)))
@@ -513,16 +536,16 @@
         return FP[item] if UA[item] is None else UA[item]
 
     def g_send(item, z, step):
-        src = ready(item) if z is None else OUT[item].at[z * n_y + my_y]
+        src = ready(item) if z is None else out_at(item, z * n_y + my_y)
         at = my_z if z is None else z
-        dst = OUT[item].at[at * n_y + my_y]
+        dst = out_at(item, at * n_y + my_y)
         return remote(src, dst, gs.at[item, (step + 1) // 2, at], gr.at[item, at],
                       (me_f, (my_z + step) * n_y + my_y))
 
     def h_send(item, z):
-        src = ready(item) if z is None else OUT[item].at[z * n_y + my_y]
+        src = ready(item) if z is None else out_at(item, z * n_y + my_y)
         at = my_z if z is None else z
-        return remote(src, OUT[item].at[at * n_y + my_y], hs.at[item, at], hr.at[item, at],
+        return remote(src, out_at(item, at * n_y + my_y), hs.at[item, at], hr.at[item, at],
                       (me_f, my_z * n_y + other_y))
 
     def spread(item):
@@ -535,7 +558,7 @@
             g_send(item, None, -1).start()
 
         h_send(item, None).start()
-        pltpu.make_async_copy(ready(item), OUT[item].at[me_c], own.at[item]).start()
+        pltpu.make_async_copy(ready(item), out_at(item, me_c), own.at[item]).start()
 
     def pass_on(item, far):
         for step in (1, -1):
@@ -566,29 +589,38 @@
                     g_send(item, z, step).wait_send()
 
         for z in range(n_z):
-            src = OUT[item].at[z * n_y + other_y]
+            src = out_at(item, z * n_y + other_y)
             cp = remote(src, src, hs.at[item, z], hr.at[item, z], (me_f, my_z * n_y + other_y))
             cp.wait_send()
             cp.wait_recv()
-        pltpu.make_async_copy(ready(item), OUT[item].at[me_c], own.at[item]).wait()
+        pltpu.make_async_copy(ready(item), out_at(item, me_c), own.at[item]).wait()
 
     lax.fori_loop(0, width // 256, down_grad, 0)
-    for k in range(n_z):
-        y_start(0, k)
+    for item in DOWN:
+        for k in range(n_z):
+            y_start(item, k)
+    lax.fori_loop(0, n_f, mlp_backward, 0)
     lax.fori_loop(0, width // 256, up_grad, 0)
-    for k in range(n_z):
-        y_start(1, k)
+    for item in UP:
+        for k in range(n_z):
+            y_start(item, k)
+
+    def sums(item, steps=range(n_c // n_y - 1)):
+        for k in steps:
+            y_sum(item, k)
+
+    far_first, nearer = range(1), range(1, n_c // n_y - 1)
 
     at_end = jnp.logical_or(my_z == 0, my_z == last)
     between = jnp.logical_and(my_z > 0, my_z < last)
 
+    heads_arrival(0)
+    heads_arrival(2)
+
     @pl.when(at_end)
     def _():
-        for k in range(last):
-            y_sum(0, k)
-
-    heads_arrival(0)
-    heads_arrival(2)
+        sums(0)
+
     heads_arrival(1)
     attention_setup(AQ, AG, AS, KT, VT, GT, CB)
 
@@ -605,11 +637,11 @@
         def queries_step(t, inner):
             lax.switch((me_c + 1 + t) % n_c, [queries_of(i, h) for i in range(n_c)])
             give(0, h, t)
-            for n, at in enumerate(SUM_AT):
-
-                @pl.when(jnp.logical_and(h * n_c + t == at, between))
-                def _(n=n):
-                    y_sum(0, n)
+            for at, where, item, steps in SUMS_IN:
+
+                @pl.when(jnp.logical_and(h * n_c + t == at, at_end if where == 0 else between))
+                def _(item=item, steps=steps):
+                    sums(item, steps)
 
             return inner
 
@@ -621,13 +653,14 @@
         return carry
 
     lax.fori_loop(0, 2, one_head, 0)
-    piece_total(0)
-    spread(0)
+    for item in DOWN:
+        piece_total(item)
+        spread(item)
 
     @pl.when(at_end)
     def _():
-        for k in range(last):
-            y_sum(1, k)
+        for item in UP:
+            sums(item)
 
     ROWS[...] = jnp.zeros_like(ROWS)
     for j in range(n_f):
@@ -657,12 +690,15 @@
     lax.fori_loop(0, n_f, out_chunk, 0)
     GN[...] = tn(CX[...].reshape(total, cut), DY[...].reshape(total, width)).astype(bf16).reshape(n_c, cut // n_c, width)
     for k in range(n_z):
-        y_start(2, k)
-    pass_on(0, 1)
+        y_start(4, k)
 
     @pl.when(between)
     def _():
-        y_sum(1, 0)
+        for item in UP:
+            sums(item, far_first)
+
+    pass_on(0, 1)
+    pass_on(1, 1)
 
     back_arrival(1, 0)
     back_arrival(1, 1)
@@ -684,11 +720,6 @@
         ES[0:1, :] += jnp.sum(e * XH[s].astype(f32), axis=0, keepdims=True)
         ES[1:2, :] += jnp.sum(e, axis=0, keepdims=True)
         H2[s] = (e * ROWS[0:1, :] + H2[s].astype(f32)).astype(bf16)
-
-        @pl.when(d != 0)
-        def _():
-            f_rows(1, d, H2, HR).start()
-
         return carry
 
     lax.fori_loop(0, n_f, mixed_chunk, 0)
@@ -697,40 +728,70 @@
     def qkv_grad(r, carry):
         at = pl.ds(pl.multiple_of(r * tile, tile), tile)
         res = tn(N1[:, :, at].reshape(total, tile), N2[:, :, 0:qc].reshape(total, qc)).astype(bf16)
-        GQ[:, r] = res.reshape(n_c, tile // n_c, qc)
+        res = res.reshape(n_c, 2, tile // n_c // 2, qc)
+        for i in range(2):
+            GQ[i, :, r] = res[:, i]
         return carry
 
     lax.fori_loop(0, n_f, qkv_grad, 0)
-    for k in range(n_z):
-        y_start(3, k)
+    for item in QKV:
+        for k in range(n_z):
+            y_start(item, k)
 
     for j in range(n_f):
         S1[j, 0:2, :] = ES[0:2, j * tile : (j + 1) * tile]
         S1[j, 2:4, :] = SMALL[2:4, j * tile : (j + 1) * tile]
         S1[j, 4:8, :] = jnp.zeros((4, tile), f32)
     for d in range(1, n_f):
-        f_rows(3, d, S1, R1).start()
+        f_rows(2, d, S1, R1).start()
 
     @pl.when(between)
     def _():
-        y_sum(1, 1)
-        y_sum(1, 2)
-
-    for k in range(last):
-        y_sum(2, k)
+        for item in UP:
+            sums(item, nearer)
+        sums(4, far_first)
+
+    @pl.when(at_end)
+    def _():
+        sums(4)
+
     pass_on(0, 2)
-    piece_total(1)
-    f_start(1)
+    pass_on(1, 2)
+    for item in UP:
+        piece_total(item)
+        f_start(item)
+
+    @pl.when(between)
+    def _():
+        sums(4, nearer)
+        sums(5, far_first)
+
+    @pl.when(at_end)
+    def _():
+        sums(5)
+
     pass_on(0, 3)
-    for k in range(last):
-        y_sum(3, k)
-    piece_total(2)
-    spread(2)
-    f_wait(1)
-    spread(1)
-
+    pass_on(1, 3)
     for d in range(1, n_f):
-        f_rows(3, d, S1, R1).wait_recv()
+        f_rows(1, d, H2, HR).start()
+    for item in UP:
+        f_wait(item)
+        spread(item)
+    piece_total(4)
+    spread(4)
+
+    @pl.when(between)
+    def _():
+        sums(6, far_first)
+        sums(5, nearer)
+        sums(6, nearer)
+
+    @pl.when(at_end)
+    def _():
+        sums(6)
+
+    for d in range(1, n_f):
+        f_rows(2, d, S1, R1).wait_recv()
     S2[...] = jnp.zeros_like(S2)
     S2[0:1, 0:qc] = ES[4:5, 0:qc]
     S2[1:2, :] = SMALL[0:1, :]
@@ -747,14 +808,18 @@
     for k in range(1, n_c):
         s2_send(k).start()
 
-    piece_total(3)
-    f_start(3)
-    pass_on(1, 1)
     pass_on(2, 1)
-    f_wait(3)
-    spread(3)
-    pass_on(1, 2)
+    piece_total(5)
+    f_start(5)
+    pass_on(3, 1)
+    pass_on(4, 1)
+    piece_total(6)
+    f_start(6)
     pass_on(2, 2)
+    f_wait(5)
+    spread(5)
+    pass_on(3, 2)
+    pass_on(4, 2)
     for d in range(1, n_f):
         f_rows(0, d, PT, OR).wait_recv()
     v = X[me_f].astype(f32)
@@ -763,9 +828,12 @@
         acc = acc + OR[d - 1].astype(f32)
     out_ref[...] = acc.astype(bf16)
 
-    pass_on(3, 1)
-    pass_on(1, 3)
+    f_wait(6)
+    spread(6)
+    pass_on(5, 1)
     pass_on(2, 3)
+    pass_on(3, 3)
+    pass_on(4, 3)
     for d in range(1, n_f):
         f_rows(1, d, H2, HR).wait_recv()
     h = H2[me_f].astype(f32)
@@ -776,8 +844,11 @@
     xhat = center * rstd
     grad = rstd * (h - jnp.mean(h, axis=-1, keepdims=True) - xhat * jnp.mean(h * xhat, axis=-1, keepdims=True))
     gx_ref[...] = (DY[me_f].astype(f32) + grad).astype(bf16)
-    pass_on(3, 2)
-    pass_on(3, 3)
+    pass_on(6, 1)
+    pass_on(5, 2)
+    pass_on(6, 2)
+    pass_on(5, 3)
+    pass_on(6, 3)
     tot = S2[...]
     for k in range(1, n_c):
         s2_send(k).wait_recv()
@@ -803,10 +874,10 @@
     for d in range(1, n_f):
         f_rows(0, d, PT, OR).wait_send()
         f_rows(1, d, H2, HR).wait_send()
-        f_rows(3, d, S1, R1).wait_send()
-        f_send(1, d).wait_send()
-        f_send(3, d).wait_send()
-    for item in range(4):
+        f_rows(2, d, S1, R1).wait_send()
+        for item in UP + QKV:
+            f_send(item, d).wait_send()
+    for item in range(len(G)):
         for z in range(n_z):
             y_send(item, z).wait_send()
 
@@ -823,8 +894,8 @@
     n_z, group, cut, n = n_c // n_y, n_c // n_f, width // n_f, n_c * rows
     S, V, D = jax.ShapeDtypeStruct, pltpu.VMEM, pltpu.SemaphoreType.DMA
     pat = jnp.asarray(rotary_pattern(), bf16)
-    shapes = [(uc // n_c, width), (n_f, cut // n_c, uc), (cut // n_c, width), (n_f, cut // n_c, qc)]
-    wides = [shapes[0], (cut // n_c, n_f * uc), shapes[2], (cut // n_c, n_f * qc)]
+    shapes = [(uc // n_c // 2, width), (n_f, cut // n_c // 2, uc), (cut // n_c, width), (n_f, cut // n_c // 2, qc)]
+    wides = [shapes[0], (cut // n_c // 2, n_f * uc), shapes[2], (cut // n_c // 2, n_f * qc)]
     act = V((n_f, rows, width), bf16)
     scratch = [
         act, act, V((n_f, cut, qc), bf16), V((n_f, cut, uc), bf16), V((uc, width), bf16), V((cut, width), bf16),
@@ -835,10 +906,12 @@
         V((n_f, group, 2, rows, 128), bf16), V((n_f, group, 2, rows, 128), bf16),
         V((n_f - 1, rows, width), bf16), V((n_f - 1, rows, width), bf16), V((8, width), f32),
     ]
-    scratch += [V((n_c,) + s, bf16) for s in shapes]
-    scratch += [V((n_z,) + s, bf16) for s in shapes]
-    scratch += [V((2, n_z) + s, bf16) for s in shapes]
-    scratch += [V(s, bf16) for s in shapes] + [V(wides[1], bf16), V(wides[3], bf16)]
+    parts = [(2,), (2,), (), (2,)]
+    scratch += [V(p + (n_c,) + s, bf16) for p, s in zip(parts, shapes)]
+    scratch += [V(p + (n_z,) + s, bf16) for p, s in zip(parts, shapes)]
+    scratch += [V(p + (2, n_z) + s, bf16) for p, s in zip(parts, shapes)]
+    scratch += [V(p + s, bf16) for p, s in zip(parts, shapes)]
+    scratch += [V((2,) + wides[1], bf16), V((2,) + wides[3], bf16)]
     scratch += [V((n_f, 8, cut), f32), V((n_f - 1, 8, cut), f32), V((8, uc), f32), V((n_c, 8, uc), f32), V((8, width), f32)]
     scratch += [
         V((n_c, 3, rows, 128), bf16), V((n_c, rows, 128), bf16), V((n_c, 8, rows), f32), V((128, n), bf16), V((128, n), bf16),
@@ -847,13 +920,13 @@
     ]
     scratch += [
         D((7,)), D((5, n_f)), D((5, n_f)), D((2, 3, n_f)), D((2, 3, n_f)), D((3, n_c)), D((3, n_c)),
-        D((5, n_f)), D((5, n_f)), D((5, n_c)), D((5, n_c)),
-        D((4, n_z)), D((4, n_z)), D((4, n_z)), D((4, 2, n_z)), D((4, 2, n_z)), D((4, n_z)), D((4, n_z)), D((4, n_z)), D((4,)),
+        D((8, n_f)), D((8, n_f)), D((5, n_c)), D((5, n_c)),
+        D((7, n_z)), D((7, n_z)), D((7, n_z)), D((7, 2, n_z)), D((7, 2, n_z)), D((7, n_z)), D((7, n_z)), D((7, n_z)), D((7,)),
     ]
     return pl.pallas_call(
         functools.partial(kernel_m, n_f, n_c, n_y),
         out_shape=(S((rows, width), bf16), S((rows, width), bf16))
-        + tuple(S((n_c,) + s, bf16) for s in wides) + (S((8, uc), f32),),
+        + tuple(S((n_c,) + p + s, bf16) for p, s in zip(parts, wides)) + (S((8, uc), f32),),
         in_specs=[hbm] * 7 + [vmem] * 2,
         out_specs=(vmem, vmem) + (hbm,) * 4 + (vmem,),
         scratch_shapes=scratch,
@@ -862,7 +935,7 @@
     )(x, dy, wq, wu, wd, wn, pk, pat, vectors)
 
 
-def kernel_d(od, ou, on, oq, out, gx, vec, fd, fu, fn, fq, o1, o2, bq, b1, bu, n1g, n1b, n2g, n2b):
+def kernel_d(od, ou, on, oq, out, gx, vec, fd, fu, fn, fq, o1, o2, bq, b1, b2, bu, n1g, n1b, n2g, n2b):
     for src, dst in ((od, fd), (ou, fu), (on, fn), (oq, fq)):
         dst[...] = src[0].astype(f32)
     o1[...] = out[...]
@@ -870,7 +943,7 @@
 
     @pl.when(pl.program_id(0) == 0)
     def _():
-        for ref, row in ((bq, 0), (bu, 1), (b1, 2), (n1g, 3), (n1b, 4), (n2g, 5), (n2b, 6)):
+        for ref, row in ((bq, 0), (bu, 1), (b1, 2), (b2, 2), (n1g, 3), (n1b, 4), (n2g, 5), (n2b, 6)):
             ref[...] = vec[row, 0 : ref.shape[0]]
 
 
@@ -889,7 +962,7 @@
 
     strip = pl.BlockSpec((rows // n_c, out.shape[1]), lambda i: (i, 0))
     grads = (od, ou, on, oq)
-    sizes = (qc, cut, vec.shape[1], cut, cut, cut, cut)
+    sizes = (qc, cut, cut, vec.shape[1], cut, cut, cut, cut)
     return pl.pallas_call(
         kernel_d,
         grid=(n_c,),
@@ -924,9 +997,10 @@
                          dense_bias, down_bias, qkv_bias, up_bias)
     out, gx, od, ou, on, oq, vec = call_m(
         n_f, n_c, n_y, tokens, cotangent, qkv_weight, up_weight, down_weight, dense_weight, pk, vectors)
-    gd, gu, gn, gq, out, gx, bq, b1, bu, n1g, n1b, n2g, n2b = call_d(
+    od, ou, oq = (a.reshape(a.shape[0], -1, a.shape[3]) for a in (od, ou, oq))
+    gd, gu, gn, gq, out, gx, bq, b1, b2, bu, n1g, n1b, n2g, n2b = call_d(
         od, ou, on, oq, out, gx, vec, qkv_bias.shape[0])
-    return out, gx, gq, bq, gn, b1, gu, bu, gd, b1, n1g, n1b, n2g, n2b
+    return out, gx, gq, bq, gn, b1, gu, bu, gd, b2, n1g, n1b, n2g, n2b
 
 
 def rotary_tables(places):

time: 261 us -> 246 us (0.943)
  Pallas kernels: 259 us -> 244 us
    pallas_call x1, Pallas kernels: 248 us -> 233 us  [call_m(): pl.pallas_call(functools.partial(kernel_m, n_f, n_c, n_y), out_shape=(S((...]
where the time goes in v2:
time: 246 us; the launch traced here: 245 us
  Pallas kernels  244 us (99%)
    pallas_call x1, Pallas kernels, call_m(): pl.pallas_call(functools.partial(kernel_m, n_f, n_c, n_y), out_shape=(S((...  233 us
    pallas_call x1, Pallas kernels, call_d(): pl.pallas_call(kernel_d, grid=(n_c,), out_shape=tuple((S((n_c * a.shape[1...  9.49 us

profile of v2, /device:TPU:0, one launch (start us, length us, event | category | flops | bytes accessed | tf_op | source)
XLA Modules:
  0.0 245.2 jit_solution(1636512626694111622)
XLA Ops:
  0.6 1.5 pack.1
  2.2 233.3 %layer.1 = (bf16[256,1024]{1,0:T(8,128)(2,1)}, bf16[256,1024]{1,0:T(8,128)(2,1)}, bf16[8,2,64,1024]{3,2,1,0:T(8,128)(2,1)}, bf16[8,2,16,4096]{3,2,1,0:T(8,128)(2...) custom-call(bf16[256,1024]{1,0:T(8,128)(2,1)} %x_hbm.1, ...), custom_call_target="tpu_custom_call" | custom-call | tf_op jit(solution)/shard_map/layer/pallas_call | solution.py:926
  235.5 9.5 %widen.1 = (f32[1024,1024]{1,0:T(8,128)}, f32[256,4096]{1,0:T(8,128)}, f32[256,1024]{1,0:T(8,128)}, f32[256,3072]{1,0:T(8,128)}, bf16[256,1024]{1,0:T(8,128)(2,1...) custom-call(bf16[8,128,1024]{2,1,0:T(8,128)(2,1)} %bitcast.3, ...), custom_call_target="tpu_custom_call" | custom-call | tf_op jit(solution)/shard_map/widen/pallas_call | solution.py:966

commit v3 on v2

--- a/solution.py
+++ b/solution.py
@@ -171,7 +171,7 @@
     t_buf[rest, :] = dq * 0.125
 
 
-SUMS_IN = ((1, 0, 1, (0, 1, 2)), (4, 1, 0, (0,)), (6, 1, 1, (0,)), (9, 1, 0, (1, 2)), (12, 1, 1, (1, 2)))
+SUMS_IN = ((1, 0, 1, (0, 1, 2)), (4, 1, 0, (0,)), (5, 1, 1, (0,)), (8, 1, 0, (1, 2)), (10, 1, 1, (1, 2)))
 
 
 def kernel_m(
@@ -338,8 +338,8 @@
     first_shares(2)
     arrival(0, 1)
     norm_chunk(flipped(me_f, 1, n_f))
+    next_shares(2)
     first_shares(3)
-    next_shares(2)
     next_shares(3)
     local[2].wait()
     weights(2)
@@ -378,7 +378,6 @@
     for d in range(2, n_f, 2):
         arrival(1, d)
         forward(1, d).start()
-    lax.fori_loop(n_f // 2, n_f, mlp_forward, 0)
     local[3].wait()
     local[4].wait()
     for d in range(1, n_f, 2):
@@ -393,6 +392,7 @@
         return carry
 
     lax.fori_loop(0, n_f, gc_chunk, 0)
+    lax.fori_loop(n_f // 2, n_f, mlp_forward, 0)
 
 
     def down_grad(r, carry):
@@ -782,13 +782,34 @@
 
     @pl.when(between)
     def _():
+        sums(5, nearer)
+
+    pass_on(2, 1)
+    pass_on(3, 1)
+
+    @pl.when(at_end)
+    def _():
+        sums(6)
+
+    @pl.when(between)
+    def _():
         sums(6, far_first)
-        sums(5, nearer)
+
+    piece_total(5)
+    f_start(5)
+    pass_on(4, 1)
+
+    @pl.when(between)
+    def _():
         sums(6, nearer)
 
-    @pl.when(at_end)
-    def _():
-        sums(6)
+    pass_on(2, 2)
+    pass_on(3, 2)
+    piece_total(6)
+    f_start(6)
+    f_wait(5)
+    spread(5)
+    pass_on(4, 2)
 
     for d in range(1, n_f):
         f_rows(2, d, S1, R1).wait_recv()
@@ -808,18 +829,6 @@
     for k in range(1, n_c):
         s2_send(k).start()
 
-    pass_on(2, 1)
-    piece_total(5)
-    f_start(5)
-    pass_on(3, 1)
-    pass_on(4, 1)
-    piece_total(6)
-    f_start(6)
-    pass_on(2, 2)
-    f_wait(5)
-    spread(5)
-    pass_on(3, 2)
-    pass_on(4, 2)
     for d in range(1, n_f):
         f_rows(0, d, PT, OR).wait_recv()
     v = X[me_f].astype(f32)
@@ -827,13 +836,14 @@
     for d in range(1, n_f):
         acc = acc + OR[d - 1].astype(f32)
     out_ref[...] = acc.astype(bf16)
-
     f_wait(6)
     spread(6)
-    pass_on(5, 1)
     pass_on(2, 3)
     pass_on(3, 3)
+    pass_on(5, 1)
     pass_on(4, 3)
+    pass_on(6, 1)
+
     for d in range(1, n_f):
         f_rows(1, d, H2, HR).wait_recv()
     h = H2[me_f].astype(f32)
@@ -844,7 +854,6 @@
     xhat = center * rstd
     grad = rstd * (h - jnp.mean(h, axis=-1, keepdims=True) - xhat * jnp.mean(h * xhat, axis=-1, keepdims=True))
     gx_ref[...] = (DY[me_f].astype(f32) + grad).astype(bf16)
-    pass_on(6, 1)
     pass_on(5, 2)
     pass_on(6, 2)
     pass_on(5, 3)
@@ -937,7 +946,7 @@
 
 def kernel_d(od, ou, on, oq, out, gx, vec, fd, fu, fn, fq, o1, o2, bq, b1, b2, bu, n1g, n1b, n2g, n2b):
     for src, dst in ((od, fd), (ou, fu), (on, fn), (oq, fq)):
-        dst[...] = src[0].astype(f32)
+        dst[...] = src[...].astype(f32)
     o1[...] = out[...]
     o2[...] = gx[...]
 
@@ -948,28 +957,24 @@
 
 
 def call_d(od, ou, on, oq, out, gx, vec, qc):
-    n_c, rows, cut = od.shape[0], out.shape[0], on.shape[0] * on.shape[1]
+    steps, cut = 2, on.shape[0]
     S = jax.ShapeDtypeStruct
 
     def whole(n):
         return pl.BlockSpec((n,), lambda i: (0,))
 
     def block(a):
-        return pl.BlockSpec((1,) + a.shape[1:], lambda i: (i, 0, 0))
-
-    def flat(a):
-        return pl.BlockSpec(a.shape[1:], lambda i: (i, 0))
-
-    strip = pl.BlockSpec((rows // n_c, out.shape[1]), lambda i: (i, 0))
+        return pl.BlockSpec((a.shape[0] // steps, a.shape[1]), lambda i: (i, 0))
+
     grads = (od, ou, on, oq)
     sizes = (qc, cut, cut, vec.shape[1], cut, cut, cut, cut)
     return pl.pallas_call(
         kernel_d,
-        grid=(n_c,),
-        out_shape=tuple(S((n_c * a.shape[1], a.shape[2]), f32) for a in grads)
+        grid=(steps,),
+        out_shape=tuple(S(a.shape, f32) for a in grads)
         + (S(out.shape, bf16), S(out.shape, bf16)) + tuple(S((n,), f32) for n in sizes),
-        in_specs=[block(a) for a in grads] + [strip, strip, pl.BlockSpec(vec.shape, lambda i: (0, 0))],
-        out_specs=tuple(flat(a) for a in grads) + (strip, strip) + tuple(whole(n) for n in sizes),
+        in_specs=[block(a) for a in grads + (out, gx)] + [pl.BlockSpec(vec.shape, lambda i: (0, 0))],
+        out_specs=tuple(block(a) for a in grads + (out, gx)) + tuple(whole(n) for n in sizes),
         compiler_params=pltpu.CompilerParams(vmem_limit_bytes=62 * 2**20),
         name="widen",
     )(od, ou, on, oq, out, gx, vec)
@@ -997,7 +1002,7 @@
                          dense_bias, down_bias, qkv_bias, up_bias)
     out, gx, od, ou, on, oq, vec = call_m(
         n_f, n_c, n_y, tokens, cotangent, qkv_weight, up_weight, down_weight, dense_weight, pk, vectors)
-    od, ou, oq = (a.reshape(a.shape[0], -1, a.shape[3]) for a in (od, ou, oq))
+    od, ou, on, oq = (a.reshape(-1, a.shape[-1]) for a in (od, ou, on, oq))
     gd, gu, gn, gq, out, gx, bq, b1, b2, bu, n1g, n1b, n2g, n2b = call_d(
         od, ou, on, oq, out, gx, vec, qkv_bias.shape[0])
     return out, gx, gq, bq, gn, b1, gu, bu, gd, b2, n1g, n1b, n2g, n2b

time: 246 us -> 241 us (0.980)
  Pallas kernels: 244 us -> 240 us
    pallas_call x1, Pallas kernels: 233 us -> 230 us  [call_m(): pl.pallas_call(functools.partial(kernel_m, n_f, n_c, n_y), out_shape=(S((...]
where the time goes in v3:
time: 241 us; the launch traced here: 240 us
  Pallas kernels  240 us (100%)
    pallas_call x1, Pallas kernels, call_m(): pl.pallas_call(functools.partial(kernel_m, n_f, n_c, n_y), out_shape=(S((...  230 us
    pallas_call x1, Pallas kernels, call_d(): pl.pallas_call(kernel_d, grid=(steps,), out_shape=tuple((S(a.shape, f32)...  8.1 us

profile of v3, /device:TPU:0, one launch (start us, length us, event | category | flops | bytes accessed | tf_op | source)
XLA Modules:
  0.0 240.3 jit_solution(7203986778246386593)
XLA Ops:
  0.6 1.5 pack.1
  2.2 229.9 %layer.1 = (bf16[256,1024]{1,0:T(8,128)(2,1)}, bf16[256,1024]{1,0:T(8,128)(2,1)}, bf16[8,2,64,1024]{3,2,1,0:T(8,128)(2,1)}, bf16[8,2,16,4096]{3,2,1,0:T(8,128)(2...) custom-call(bf16[256,1024]{1,0:T(8,128)(2,1)} %x_hbm.1, ...), custom_call_target="tpu_custom_call" | custom-call | tf_op jit(solution)/shard_map/layer/pallas_call | solution.py:935
  232.1 8.1 %widen.1 = (f32[1024,1024]{1,0:T(8,128)}, f32[256,4096]{1,0:T(8,128)}, f32[256,1024]{1,0:T(8,128)}, f32[256,3072]{1,0:T(8,128)}, bf16[256,1024]{1,0:T(8,128)(2,1...) custom-call(bf16[1024,1024]{1,0:T(8,128)(2,1)} %bitcast.4, ...), custom_call_target="tpu_custom_call" | custom-call | tf_op jit(solution)/shard_map/widen/pallas_call | solution.py:971

commit v4 on v3

--- a/solution.py
+++ b/solution.py
@@ -434,14 +434,19 @@
             buf = (CT, DQ)[pair].at[src // group, src % group, h]
             remote(buf, buf, as_.at[2 * pair + h, k], ar.at[2 * pair + h, k], (me_f, src)).wait_recv()
 
+    def turn_to(t):
+        half = n_c // 2
+        return (1 - t % 2) * (half + t // 2) + t % 2 * (half - 1 - t // 2)
+
     def give(pair, h, t):
-        i = (me_c + 1 + t) % n_c
-
-        @pl.when(t < n_c - 1)
+        k = turn_to(t)
+        i = (me_c + k) % n_c
+
+        @pl.when(k != 0)
         def _():
-            back(pair, h, t + 1, i).start()
-
-        @pl.when(t == n_c - 1)
+            back(pair, h, k, i).start()
+
+        @pl.when(k == 0)
         def _():
             back_own(pair, h, i).start()
 
@@ -635,7 +640,7 @@
         DK[...] = jnp.zeros_like(DK)
 
         def queries_step(t, inner):
-            lax.switch((me_c + 1 + t) % n_c, [queries_of(i, h) for i in range(n_c)])
+            lax.switch((me_c + turn_to(t)) % n_c, [queries_of(i, h) for i in range(n_c)])
             give(0, h, t)
             for at, where, item, steps in SUMS_IN:
 

time: 241 us -> 240 us (level)
  Pallas kernels: 240 us -> 237 us
where the time goes in v4:
time: 240 us; the launch traced here: 238 us
  Pallas kernels  237 us (99%)
    pallas_call x1, Pallas kernels, call_m(): pl.pallas_call(functools.partial(kernel_m, n_f, n_c, n_y), out_shape=(S((...  228 us
    pallas_call x1, Pallas kernels, call_d(): pl.pallas_call(kernel_d, grid=(steps,), out_shape=tuple((S(a.shape, f32)...  8.1 us

profile of v4, /device:TPU:0, one launch (start us, length us, event | category | flops | bytes accessed | tf_op | source)
XLA Modules:
  0.0 238.3 jit_solution(6895702136055197279)
XLA Ops:
  0.6 1.5 pack.1
  2.2 227.8 %layer.1 = (bf16[256,1024]{1,0:T(8,128)(2,1)}, bf16[256,1024]{1,0:T(8,128)(2,1)}, bf16[8,2,64,1024]{3,2,1,0:T(8,128)(2,1)}, bf16[8,2,16,4096]{3,2,1,0:T(8,128)(2...) custom-call(bf16[256,1024]{1,0:T(8,128)(2,1)} %x_hbm.1, ...), custom_call_target="tpu_custom_call" | custom-call | tf_op jit(solution)/shard_map/layer/pallas_call | solution.py:940
  230.0 8.1 %widen.1 = (f32[1024,1024]{1,0:T(8,128)}, f32[256,4096]{1,0:T(8,128)}, f32[256,1024]{1,0:T(8,128)}, f32[256,3072]{1,0:T(8,128)}, bf16[256,1024]{1,0:T(8,128)(2,1...) custom-call(bf16[1024,1024]{1,0:T(8,128)(2,1)} %bitcast.4, ...), custom_call_target="tpu_custom_call" | custom-call | tf_op jit(solution)/shard_map/widen/pallas_call | solution.py:976
